TPU v7x, 512 devices: a whole 4x4x16 slice. The times are simulated.
512 devices in a mesh: ra: 16 (over z_lo, core), rb: 32 (over x, y, z_hi).
Axes of the slice: x: 4, y: 4, z: 16 (z_hi: 2, z_lo: 8; z = z_hi * 8 + z_lo), core: 2. Of those that a mesh axis runs over, the one named last changes fastest.
Arguments:
- amplitude: bfloat16 [2, 512, 512, 256], P(None, 'ra', 'rb'), may hold values from -6 to 6
- coupling: bfloat16 [6, 256, 256], replicated, may hold values from -0.5 to 0.5
- pattern: int32 [6, 4, 4], replicated, may hold values 0 or 1
- radial: float32 [6, 512, 512], P(None, 'ra', 'rb'), may hold values from -2.4 to 2.4
- first_prop: bfloat16 [2, 512, 512], replicated, may hold values from -0.1875 to 0.1875
- second_prop: bfloat16 [2, 512, 512], replicated, may hold values from -0.1875 to 0.1875
Outputs:
- evolved: bfloat16 [2, 512, 512, 256], P(None, 'ra', 'rb')
All inputs are finite; a program needn't handle non-finite values.
Results may differ from a plain program's by a relative error of at most 0.0095.
Values may be sent and summed in bfloat16 or wider, within the bound.
No kernel may reach another device: no remote copies, remote signals or barrier semaphores. Data moves between devices by JAX's collectives and lax.ppermute only.
A program may use at most 64 MiB of HBM per device.

v0:
```python
import jax
import jax.numpy as jnp
from jax import lax
from jax.sharding import PartitionSpec as P

KTERMS = 6
STEPS = 2


def complex_rows(matrix, piece):
    form = "ac,cqw->aqw"
    real_part = jnp.einsum(
        form, matrix[0], piece[0], preferred_element_type=jnp.float32
    ) - jnp.einsum(form, matrix[1], piece[1], preferred_element_type=jnp.float32)
    imag_part = jnp.einsum(
        form, matrix[0], piece[1], preferred_element_type=jnp.float32
    ) + jnp.einsum(form, matrix[1], piece[0], preferred_element_type=jnp.float32)
    return jnp.stack([real_part, imag_part]).astype(jnp.bfloat16)


def on_device(amplitude, coupling, pattern, radial, first_prop, second_prop):
    first_rows, second_rows, channels = (amplitude.shape[1], amplitude.shape[2], amplitude.shape[3])
    cells = first_rows * second_rows
    count = pattern.shape[1]
    block_size = channels // count
    groups_a = lax.axis_size("ra")
    groups_b = lax.axis_size("rb")
    width_a = channels // groups_a
    width_b = channels // groups_b
    spread = jnp.broadcast_to(
        pattern[:, :, None, :, None], (KTERMS, count, block_size, count, block_size)
    )
    block_mask = spread.reshape(KTERMS, channels, channels).astype(jnp.bfloat16)
    weights = coupling * block_mask
    radial_cells = radial.reshape(KTERMS, cells).T
    for sweep in range(STEPS):
        flat = amplitude.reshape(2 * cells, channels)
        applied = jnp.einsum("mj,kij->mki", flat, weights, preferred_element_type=jnp.float32)
        applied = applied.reshape(2, cells, KTERMS, channels)
        coupled = jnp.sum(applied * radial_cells[None, :, :, None], axis=2)
        wide = amplitude.reshape(2, cells, channels).astype(jnp.float32)
        kicked = jnp.stack([wide[0] + coupled[1], wide[1] - coupled[0]]).astype(jnp.bfloat16)
        grouped = kicked.reshape(2, first_rows, second_rows, groups_a, width_a)
        grouped = grouped.transpose(0, 1, 3, 2, 4).reshape(
            2, first_rows, groups_a, second_rows * width_a
        )
        half = complex_rows(
            first_prop, lax.all_to_all(grouped, "ra", split_axis=2, concat_axis=1, tiled=True)
        )
        restored = lax.all_to_all(half, "ra", split_axis=1, concat_axis=2, tiled=True)
        restored = restored.reshape(2, first_rows, groups_a, second_rows, width_a)
        restored = restored.transpose(0, 1, 3, 2, 4).reshape(
            2, first_rows, second_rows, groups_b, width_b
        )
        regrouped = restored.transpose(0, 2, 3, 1, 4).reshape(
            2, second_rows, groups_b, first_rows * width_b
        )
        moved = complex_rows(
            second_prop, lax.all_to_all(regrouped, "rb", split_axis=2, concat_axis=1, tiled=True)
        )
        settled = lax.all_to_all(moved, "rb", split_axis=1, concat_axis=2, tiled=True)
        settled = settled.reshape(2, second_rows, groups_b, first_rows, width_b)
        amplitude = settled.transpose(0, 3, 1, 2, 4).reshape(2, first_rows, second_rows, channels)
    return amplitude


def solution(mesh):
    return jax.shard_map(
        on_device,
        mesh=mesh,
        in_specs=(P(None, "ra", "rb", None), P(), P(), P(None, "ra", "rb"), P(), P()),
        out_specs=P(None, "ra", "rb", None),
        check_vma=False,
    )
```

profile of v0, /device:TPU:33, one launch (start us, length us, event | category | flops | bytes accessed | tf_op | source)
XLA Modules:
  0.0 392.4 jit_solution(13390313931684241986)
XLA Ops:
  0.0 0.7 convert_element_type.55
  0.8 0.9 copy.141
  1.9 1.2 fusion.71
  3.5 0.5 broadcast_in_dim.2
  3.9 1.7 convert_element_type.56
  5.7 2.5 fusion
  8.7 1.4 stack.55
  10.1 2.4 stack.54
  12.6 4.5 %maximum_bitcast_fusion = bf16[2,32,16,16,16]{4,2,3,1,0:T(8,128)(2,1)} fusion(bf16[1,32,16,16,16]{4,3,2,1,0:T(8,128)(2,1)S(1)} %stack.55, bf16[1,32,16,16,16]{4,3,2,1,0:T(8,128)(2,1)} %stack.54), kind=kLoop, calls=%fused_computation.3 | loop fusion | flops 262144 | bytes 1048576 | tf_op jit(solution)/shard_map/transpose | solution.py:44
  17.1 5.5 %copy.146 = bf16[2,32,16,16,16]{1,4,3,2,0:T(8,128)(2,1)S(1)} copy(bf16[2,32,16,16,16]{4,2,3,1,0:T(8,128)(2,1)} %maximum_bitcast_fusion) | data formatting | bytes 1048576 | tf_op jit(solution)/shard_map/transpose | solution.py:44
  22.6 0.8 copy.147
  23.4 39.6 %all_to_all.120 = bf16[2,32,16,256]{3,1,0,2:T(8,128)(2,1)S(1)} all-to-all(bf16[2,32,16,256]{3,1,0,2:T(8,128)(2,1)S(1)} %copy.147), channel_id=1, replica_groups=mesh['ra'=16,'rb'=32] {'ra'}, dimensions={2} | all-to-all | bytes 1048576 | tf_op jit(solution)/shard_map/all_to_all | solution.py:48
  63.8 0.4 fusion.15
  64.5 0.5 copy.149
  65.0 33.1 %all_to_all.121 = bf16[2,512,1,256]{3,0,2,1:T(2,128)(2,1)S(1)} all-to-all(bf16[2,512,1,256]{3,0,2,1:T(2,128)(2,1)S(1)} %copy.149), channel_id=1, replica_groups=mesh['ra'=16,'rb'=32] {'ra'}, dimensions={1} | all-to-all | bytes 1048576 | tf_op jit(solution)/shard_map/all_to_all | solution.py:50
  98.1 0.9 copy.150
  99.0 1.9 copy.151
  100.9 1.9 copy.152
  102.9 3.7 copy.153
  106.6 1.8 copy.154
  108.4 50.7 %all_to_all.122 = bf16[2,16,32,256]{3,1,0,2:T(8,128)(2,1)S(1)} all-to-all(bf16[2,16,32,256]{3,1,0,2:T(8,128)(2,1)} %copy.154), channel_id=1, replica_groups=mesh['ra'=16,'rb'=32] {'rb'}, dimensions={2} | all-to-all | bytes 1048576 | tf_op jit(solution)/shard_map/all_to_all | solution.py:59
  160.6 0.5 copy.156
  161.1 27.8 %all_to_all.123 = bf16[2,512,1,256]{3,0,2,1:T(2,128)(2,1)S(1)} all-to-all(bf16[2,512,1,256]{3,0,2,1:T(2,128)(2,1)S(1)} %copy.156), channel_id=1, replica_groups=mesh['ra'=16,'rb'=32] {'rb'}, dimensions={1} | all-to-all | bytes 1048576 | tf_op jit(solution)/shard_map/all_to_all | solution.py:61
  189.0 1.9 copy.158
  190.8 8.9 %copy.159 = bf16[2,32,16,32,8]{2,1,4,3,0:T(8,128)(2,1)} copy(bf16[2,32,16,32,8]{3,4,1,2,0:T(8,128)(2,1)} %bitcast.192) | data formatting | bytes 1048576 | tf_op jit(solution)/shard_map/transpose | solution.py:63
  199.7 7.8 %reshape_reshape.4 = bf16[2,512,256]{1,2,0:T(8,128)(2,1)S(1)} reshape(bf16[2,32,16,32,8]{2,1,4,3,0:T(8,128)(2,1)} %copy.159) | data formatting | bytes 1048576 | tf_op jit(solution)/shard_map/reshape;reshape | solution.py:41
  207.6 3.8 multiply_reduce_fusion
  211.7 1.1 copy-done.3
  213.0 2.4 stack.63
  215.4 2.4 stack.64
  217.8 5.1 %maximum_bitcast_fusion.1 = bf16[2,32,16,16,16]{4,2,3,1,0:T(8,128)(2,1)} fusion(bf16[1,32,16,16,16]{4,3,2,1,0:T(8,128)(2,1)} %stack.64, bf16[1,32,16,16,16]{4,3,2,1,0:T(8,128)(2,1)} %stack.63), kind=kLoop, calls=%fused_computation.4 | loop fusion | flops 262144 | bytes 1048576 | tf_op jit(solution)/shard_map/transpose | solution.py:44
  222.9 6.5 %copy.162 = bf16[2,32,16,16,16]{1,4,3,2,0:T(8,128)(2,1)} copy(bf16[2,32,16,16,16]{4,2,3,1,0:T(8,128)(2,1)} %maximum_bitcast_fusion.1) | data formatting | bytes 1048576 | tf_op jit(solution)/shard_map/transpose | solution.py:44
  229.4 1.9 copy.163
  231.3 36.3 %all_to_all.124 = bf16[2,32,16,256]{3,1,0,2:T(8,128)(2,1)S(1)} all-to-all(bf16[2,32,16,256]{3,1,0,2:T(8,128)(2,1)S(1)} %copy.163), channel_id=1, replica_groups=mesh['ra'=16,'rb'=32] {'ra'}, dimensions={2} | all-to-all | bytes 1048576 | tf_op jit(solution)/shard_map/all_to_all | solution.py:48
  268.7 0.4 fusion.12
  269.1 0.5 copy.165
  269.6 33.1 %all_to_all.125 = bf16[2,512,1,256]{3,0,2,1:T(2,128)(2,1)S(1)} all-to-all(bf16[2,512,1,256]{3,0,2,1:T(2,128)(2,1)S(1)} %copy.165), channel_id=1, replica_groups=mesh['ra'=16,'rb'=32] {'ra'}, dimensions={1} | all-to-all | bytes 1048576 | tf_op jit(solution)/shard_map/all_to_all | solution.py:50
  302.8 1.8 copy.167
  304.5 3.5 copy.168
  308.1 4.5 %copy.169 = bf16[2,16,32,32,8]{2,4,3,1,0:T(8,128)(2,1)} copy(bf16[2,16,32,32,8]{3,4,2,1,0:T(8,128)(2,1)} %bitcast.201) | data formatting | bytes 1048576 | tf_op jit(solution)/shard_map/transpose | solution.py:55
  312.6 2.1 copy.170
  314.7 40.8 %all_to_all.126 = bf16[2,16,32,256]{3,1,0,2:T(8,128)(2,1)S(1)} all-to-all(bf16[2,16,32,256]{3,1,0,2:T(8,128)(2,1)S(1)} %copy.170), channel_id=1, replica_groups=mesh['ra'=16,'rb'=32] {'rb'}, dimensions={2} | all-to-all | bytes 1048576 | tf_op jit(solution)/shard_map/all_to_all | solution.py:59
  356.3 0.4 fusion.9
  357.1 0.5 copy.172
  357.6 27.6 %all_to_all.127 = bf16[2,512,1,256]{3,0,2,1:T(2,128)(2,1)S(1)} all-to-all(bf16[2,512,1,256]{3,0,2,1:T(2,128)(2,1)S(1)} %copy.172), channel_id=1, replica_groups=mesh['ra'=16,'rb'=32] {'rb'}, dimensions={1} | all-to-all | bytes 1048576 | tf_op jit(solution)/shard_map/all_to_all | solution.py:61
  385.2 1.1 copy.174
  386.4 3.2 copy.175
  389.6 2.8 copy.176
  (49 shorter events, 6.9 us)
Async XLA Ops:
  3.4 2.2 copy-start.2
  23.4 39.7 %copy-start = (bf16[2,512,512]{2,1,0:T(8,128)(2,1)S(1)}, bf16[2,512,512]{2,1,0:T(8,128)(2,1)}, u32[]{:S(2)}) copy-start(bf16[2,512,512]{2,1,0:T(8,128)(2,1)} %param.10) | copy-start | bytes 3145732
  108.3 50.8 %copy-start.1 = (bf16[2,512,512]{2,1,0:T(8,128)(2,1)S(1)}, bf16[2,512,512]{2,1,0:T(8,128)(2,1)}, u32[]{:S(2)}) copy-start(bf16[2,512,512]{2,1,0:T(8,128)(2,1)} %param.11) | copy-start | bytes 3145732
  199.7 7.9 %copy-start.4 = (bf16[6,256,256]{2,1,0:T(8,128)(2,1)S(1)}, bf16[6,256,256]{2,1,0:T(8,128)(2,1)}, u32[]{:S(2)}) copy-start(bf16[6,256,256]{2,1,0:T(8,128)(2,1)} %convert_element_type.56) | copy-start | bytes 2359300
  211.6 1.2 copy-start.3
where the time goes:
time: 394 us; the launch traced here: 392 us
  blocking collectives  289 us (73%)
  local copies, waits for them, and re-layouts  80.1 us (20%)
  matrix products  11.8 us (3%)
  other arithmetic  11 us (3%)
    all_to_all x2, blocking collectives, on_device(): lax.all_to_all(regrouped, 'rb', split_axis=2, concat_axis=1, tiled=True)  91.5 us
    all_to_all x2, blocking collectives, on_device(): lax.all_to_all(grouped, 'ra', split_axis=2, concat_axis=1, tiled=True)  75.8 us
    all_to_all x2, blocking collectives, on_device(): lax.all_to_all(half, 'ra', split_axis=1, concat_axis=2, tiled=True)  66.3 us
    all_to_all x2, blocking collectives, on_device(): lax.all_to_all(moved, 'rb', split_axis=1, concat_axis=2, tiled=True)  55.4 us
    transpose x2, local copies, waits for them, and re-layouts, on_device(): settled.transpose(0, 3, 1, 2, 4)  12.1 us
    transpose x2, local copies, waits for them, and re-layouts, on_device(): grouped.transpose(0, 1, 3, 2, 4)  12 us
    transpose x2, other arithmetic, on_device(): grouped.transpose(0, 1, 3, 2, 4)  9.59 us
    another operation x4, local copies, waits for them, and re-layouts, on_device(): jnp.stack([wide[0] + coupled[1], wide[1] - coupled[0]]).astype(jnp.bfloat16)  8.74 us

commit v1 on v0

v1 whole, which is shorter than its diff:
```python
import functools

import jax
import jax.numpy as jnp
from jax import lax
from jax.experimental import pallas as pl
from jax.experimental.pallas import tpu as pltpu
from jax.sharding import PartitionSpec as P

LANES = 128
BF16 = jnp.bfloat16
F32 = jnp.float32


def dot(left, right):
    return jnp.dot(left, right, preferred_element_type=F32)


def dot_rows(left, right):
    return lax.dot_general(left, right, (((1,), (1,)), ((), ())), preferred_element_type=F32)


def swap_blocks(tiles, width):
    count = len(tiles)
    per_tile = LANES // width
    bits = per_tile.bit_length() - 1
    lane = lax.broadcasted_iota(jnp.int32, tiles[0][0].shape, 1)
    for bit in range(bits):
        step = 1 << bit
        shift = width * step
        keep = (lane & shift) == 0
        fresh = list(tiles)
        for m in range(count):
            if m & step:
                continue
            low, high = tiles[m], tiles[m + step]
            fresh[m] = [jnp.where(keep, a, pltpu.roll(b, shift, 1)) for a, b in zip(low, high)]
            fresh[m + step] = [
                jnp.where(keep, pltpu.roll(a, LANES - shift, 1), b) for a, b in zip(low, high)
            ]
        tiles = fresh
    halves = count // per_tile
    return [
        [tiles[h * per_tile + m % per_tile][m // per_tile] for h in range(halves)]
        for m in range(count)
    ]


def masked_weights(coupling_ref, pattern_ref, term, block):
    channels = coupling_ref.shape[1]
    count = channels // block
    lane = lax.broadcasted_iota(jnp.int32, (block, channels), 1)
    rows = []
    for i in range(count):
        mask = jnp.zeros((block, channels), F32)
        for j in range(count):
            inside = (lane >= j * block) & (lane < (j + 1) * block)
            mask = jnp.where(inside, pattern_ref[term, i * count + j].astype(F32), mask)
        piece = coupling_ref[term, i * block:(i + 1) * block, :].astype(F32) * mask
        rows.append(piece.astype(BF16))
    return jnp.concatenate(rows, axis=0)


def kick_into(real, imag, coupling_ref, pattern_ref, factors, block, store):
    terms = coupling_ref.shape[0]
    weights = [masked_weights(coupling_ref, pattern_ref, k, block) for k in range(terms)]
    rows = real.shape[0]
    step = 128
    for start in range(0, rows, step):
        re = real[start:start + step, :]
        im = imag[start:start + step, :]
        sum_re = jnp.zeros(re.shape, F32)
        sum_im = jnp.zeros(re.shape, F32)
        for k in range(terms):
            factor = factors[start:start + step, k:k + 1]
            sum_re = sum_re + dot_rows(re, weights[k]) * factor
            sum_im = sum_im + dot_rows(im, weights[k]) * factor
        store(start, step, re.astype(F32) + sum_im, im.astype(F32) - sum_re)


def first_kick_kernel(groups, cols, amp_ref, coupling_ref, pattern_ref, radial_ref, out_ref, held):
    cells = amp_ref.shape[0] // 2
    channels = amp_ref.shape[1]
    block = channels // 4
    factors = radial_ref[...].T

    def store(start, step, re, im):
        for h in range(channels // LANES):
            held[h, start:start + step, :] = re[:, h * LANES:(h + 1) * LANES]
            held[h, cells + start:cells + start + step, :] = im[:, h * LANES:(h + 1) * LANES]

    kick_into(amp_ref[:cells, :], amp_ref[cells:, :], coupling_ref, pattern_ref, factors, block, store)
    width = channels // groups
    rows = cells // cols
    for part in range(2):
        for a in range(0, rows, 16):
            tiles = []
            for b in range(cols):
                place = pl.ds(part * cells + a * cols + b, 16, stride=cols)
                tiles.append([held[h, place, :] for h in range(channels // LANES)])
            tiles = swap_blocks(tiles, width)
            for g in range(groups):
                out_ref[g, part * rows + a:part * rows + a + 16, :] = jnp.concatenate(
                    tiles[g], axis=1
                ).astype(BF16)


def complex_dot(p_re, p_im, k_re, k_im):
    return dot(p_re, k_re) - dot(p_im, k_im), dot(p_re, k_im) + dot(p_im, k_re)


def first_forward_kernel(prop_ref, piece_ref, out_ref):
    groups, double, lanes = piece_ref.shape
    rows = double // 2
    k_re = piece_ref[:, :rows, :].reshape(groups * rows, lanes)
    k_im = piece_ref[:, rows:, :].reshape(groups * rows, lanes)
    re, im = complex_dot(prop_ref[0], prop_ref[1], k_re, k_im)
    out_ref[:, :lanes] = re.astype(BF16)
    out_ref[:, lanes:] = im.astype(BF16)


def first_back_kernel(prop_ref, piece_ref, out_ref):
    groups, double, lanes = out_ref.shape
    rows = double // 2
    re, im = complex_dot(prop_ref[0], prop_ref[1], piece_ref[:, :lanes], piece_ref[:, lanes:])
    out_ref[:, :rows, :] = re.astype(BF16).reshape(groups, rows, lanes)
    out_ref[:, rows:, :] = im.astype(BF16).reshape(groups, rows, lanes)


def order_kernel(outer, inner, prop_ref, in_ref, out_ref):
    size = prop_ref.shape[1]
    row = lax.broadcasted_iota(jnp.int32, (size, size), 0)
    col = lax.broadcasted_iota(jnp.int32, (size, size), 1)
    place = (row % outer) * inner + row // outer
    move = jnp.where(col == place, 1.0, 0.0).astype(BF16)
    for part in range(2):
        in_ref[part] = dot_rows(prop_ref[part], move).astype(BF16)
        out_ref[part] = dot(move, prop_ref[part]).astype(BF16)


def second_kernel(groups, cols, piece_ref, in_prop_ref, out_prop_ref, coupling_ref, pattern_ref,
                  radial_ref, out_ref, state, kicked):
    channels = coupling_ref.shape[1]
    block = channels // 4
    width = channels // groups
    peers = piece_ref.shape[0] // groups
    lanes = cols * width
    size = peers * cols
    for part in range(2):
        for s in range(0, peers, 16):
            tiles = []
            for g in range(groups):
                piece = piece_ref[g * peers + s:g * peers + s + 16, part * lanes:(part + 1) * lanes]
                piece = piece.astype(F32)
                tiles.append([piece[:, h * LANES:(h + 1) * LANES] for h in range(lanes // LANES)])
            tiles = swap_blocks(tiles, width)
            for b in range(cols):
                state[part, b * peers + s:b * peers + s + 16, :] = jnp.concatenate(
                    tiles[b], axis=1
                ).astype(BF16)
    re, im = complex_dot(in_prop_ref[0], in_prop_ref[1], state[0], state[1])
    factors = radial_ref[...].T

    def store(start, step, new_re, new_im):
        kicked[0, start:start + step, :] = new_re.astype(BF16)
        kicked[1, start:start + step, :] = new_im.astype(BF16)

    kick_into(re.astype(BF16), im.astype(BF16), coupling_ref, pattern_ref, factors, block, store)
    re, im = complex_dot(out_prop_ref[0], out_prop_ref[1], kicked[0], kicked[1])
    state[0] = re.astype(BF16)
    state[1] = im.astype(BF16)
    for part in range(2):
        for s in range(0, peers, 16):
            tiles = []
            for b in range(cols):
                piece = state[part, b * peers + s:b * peers + s + 16, :].astype(F32)
                tiles.append([piece[:, h * LANES:(h + 1) * LANES] for h in range(channels // LANES)])
            tiles = swap_blocks(tiles, width)
            for g in range(groups):
                out_ref[g * peers + s:g * peers + s + 16, part * lanes:(part + 1) * lanes] = (
                    jnp.concatenate(tiles[g], axis=1).astype(BF16)
                )


def last_kernel(groups, cols, piece_ref, out_ref, held):
    channels = out_ref.shape[1]
    cells = out_ref.shape[0] // 2
    rows = cells // cols
    width = channels // groups
    lanes = piece_ref.shape[2]
    for part in range(2):
        for a in range(0, rows, 16):
            tiles = []
            for g in range(groups):
                piece = piece_ref[g, part * rows + a:part * rows + a + 16, :].astype(F32)
                tiles.append([piece[:, h * LANES:(h + 1) * LANES] for h in range(lanes // LANES)])
            tiles = swap_blocks(tiles, width)
            for b in range(cols):
                place = pl.ds(part * cells + a * cols + b, 16, stride=cols)
                for h in range(channels // LANES):
                    held[h, place, :] = tiles[b][h]
    for h in range(channels // LANES):
        out_ref[:, h * LANES:(h + 1) * LANES] = held[h].astype(BF16)


def on_device(amplitude, coupling, pattern, radial, first_prop, second_prop):
    _, rows, cols, channels = amplitude.shape
    cells = rows * cols
    terms, count = pattern.shape[0], pattern.shape[1]
    groups, peers = lax.axis_size("ra"), lax.axis_size("rb")
    width = channels // groups
    lanes = cols * width
    r1, r2 = first_prop.shape[1], second_prop.shape[1]
    params = pltpu.CompilerParams(vmem_limit_bytes=48 * 1024 * 1024)
    vmem = pl.BlockSpec(memory_space=pltpu.VMEM)
    smem = pl.BlockSpec(memory_space=pltpu.SMEM)
    call = functools.partial(pl.pallas_call, compiler_params=params, out_specs=vmem)
    shape = jax.ShapeDtypeStruct
    flat_pattern = pattern.reshape(terms, count * count)

    pad = (-terms) % 8
    here = jnp.pad(radial.reshape(terms, cells), ((0, pad), (0, 0)))
    there = lax.all_to_all(radial, "rb", split_axis=1, concat_axis=2, tiled=True)
    there = jnp.pad(there.reshape(terms, r2), ((0, pad), (0, 0)))

    piece = call(
        functools.partial(first_kick_kernel, groups, cols),
        out_shape=shape((groups, 2 * rows, lanes), BF16),
        in_specs=[vmem, vmem, smem, vmem],
        scratch_shapes=[pltpu.VMEM((channels // LANES, 2 * cells, LANES), F32)],
    )(amplitude.reshape(2 * cells, channels), coupling, flat_pattern, here)
    ordered = pl.pallas_call(
        functools.partial(order_kernel, peers, cols),
        out_shape=[shape((2, r2, r2), BF16)] * 2,
        in_specs=[vmem],
        out_specs=[vmem, vmem],
        compiler_params=params,
    )(second_prop)
    piece = lax.all_to_all(piece, "ra", split_axis=0, concat_axis=0, tiled=True)
    half = call(
        first_forward_kernel,
        out_shape=shape((r1, 2 * lanes), BF16),
        in_specs=[vmem, vmem],
    )(first_prop, piece)
    half = lax.all_to_all(half, ("ra", "rb"), split_axis=0, concat_axis=0, tiled=True)
    half = call(
        functools.partial(second_kernel, groups, cols),
        out_shape=shape((groups * peers, 2 * lanes), BF16),
        in_specs=[vmem, vmem, vmem, vmem, smem, vmem],
        scratch_shapes=[pltpu.VMEM((2, r2, channels), BF16)] * 2,
    )(half, *ordered, coupling, flat_pattern, there)
    half = lax.all_to_all(half, ("ra", "rb"), split_axis=0, concat_axis=0, tiled=True)
    piece = call(
        first_back_kernel,
        out_shape=shape((groups, 2 * rows, lanes), BF16),
        in_specs=[vmem, vmem],
    )(first_prop, half)
    piece = lax.all_to_all(piece, "ra", split_axis=0, concat_axis=0, tiled=True)
    out = call(
        functools.partial(last_kernel, groups, cols),
        out_shape=shape((2 * cells, channels), BF16),
        in_specs=[vmem],
        scratch_shapes=[pltpu.VMEM((channels // LANES, 2 * cells, LANES), F32)],
    )(piece)
    return out.reshape(2, rows, cols, channels)


def solution(mesh):
    return jax.shard_map(
        on_device,
        mesh=mesh,
        in_specs=(P(None, "ra", "rb", None), P(), P(), P(None, "ra", "rb"), P(), P()),
        out_specs=P(None, "ra", "rb", None),
        check_vma=False,
    )
```

time: 394 us -> 216 us (0.55)
  the two profiles are of different devices: /device:TPU:33 before, /device:TPU:1 now
where the time goes in v1:
time: 216 us; the launch traced here: 215 us
  blocking collectives  73.8 us (34%)
  waiting for transfers between devices  68.9 us (32%)
  starting transfers between devices  41.1 us (19%)
  local copies, waits for them, and re-layouts  15.1 us (7%)
  Pallas kernels  13.7 us (6%)
    all_to_all x1, blocking collectives, on_device(): lax.all_to_all(half, ('ra', 'rb'), split_axis=0, concat_axis=0, tiled=True)  43.8 us
    all_to_all x1, blocking collectives, on_device(): piece = lax.all_to_all(piece, 'ra', split_axis=0, concat_axis=0, tiled=True)  29.9 us
    all_to_all x1, waiting for transfers between devices, on_device(): lax.all_to_all(half, ('ra', 'rb'), split_axis=0, concat_axis=0, tiled=True)  29.9 us
    all_to_all x1, waiting for transfers between devices, on_device(): piece = lax.all_to_all(piece, 'ra', split_axis=0, concat_axis=0, tiled=True)  25.4 us
    all_to_all x1, starting transfers between devices, on_device(): piece = lax.all_to_all(piece, 'ra', split_axis=0, concat_axis=0, tiled=True)  14.2 us
    all_to_all x1, starting transfers between devices, on_device(): lax.all_to_all(half, ('ra', 'rb'), split_axis=0, concat_axis=0, tiled=True)  14.2 us
    all_to_all x1, waiting for transfers between devices, on_device(): lax.all_to_all(radial, 'rb', split_axis=1, concat_axis=2, tiled=True)  13.6 us
    unnamed x24, local copies, waits for them, and re-layouts  13.5 us
  transfers between devices with their start and end apart: 3, of which 3 were waited for; matrix products, arithmetic and copies ran while one was open for 2% of the time, Pallas kernels for 1%

profile of v1, /device:TPU:1, one launch (start us, length us, event | category | flops | bytes accessed | tf_op | source)
XLA Modules:
  0.0 214.9 jit_solution(17872036054784373932)
XLA Ops:
  0.0 0.8 copy.23.pattern_ref
  0.8 0.9 copy.22
  1.7 0.1 reshape.25
  1.8 0.0 copy-start.1
  1.8 1.1 copy-done.1
  2.9 0.0 copy-start.6
  2.9 1.0 copy-done.6
  4.0 0.0 copy-start.7
  4.0 4.1 %shard_map.64 = bf16[16,64,256]{2,1,0:T(8,128)(2,1)} custom-call(bf16[1024,256]{1,0:T(8,128)(2,1)S(1)} %bitcast.15, bf16[6,256,256]{2,1,0:T(8,128)(2,1)S(1)} %copy-done.1, s32[6,16]{1,0:T(8,128)S(1)} %copy.23.pattern_ref, f32[8,512]{1,0:T(8,128)S(1)} %pad.7.radial_ref), custom_call_target="tpu_custom_call" | custom-call | tf_op jit(solution)/shard_map/pallas_call | solution.py:226
  8.1 0.0 copy-start
  8.1 14.2 %all-to-all-start = ((bf16[16,64,256]{2,1,0:T(8,128)(2,1)}), bf16[16,64,256]{2,1,0:T(8,128)(2,1)S(1)}, u32[]{:S(2)}, u32[]{:S(2)}) async-start(bf16[16,64,256]{2,1,0:T(8,128)(2,1)} %shard_map.64), calls=%async_computation | async-start | bytes 1048576 | tf_op jit(solution)/shard_map/all_to_all | solution.py:239
  22.3 0.0 copy-done.7
  22.3 0.7 copy.25
  23.0 25.4 %all-to-all-done.piece_ref = bf16[16,64,256]{2,1,0:T(8,128)(2,1)S(1)} async-done(((bf16[16,64,256]{2,1,0:T(8,128)(2,1)}), bf16[16,64,256]{2,1,0:T(8,128)(2,1)S(1)}, u32[]{:S(2)}, u32[]{:S(2)}) %all-to-all-start) | async-done | bytes 524320 | tf_op jit(solution)/shard_map/all_to_all | solution.py:239
  48.4 12.8 %all-to-all-start.2 = ((f32[6,32,16]{2,0,1:T(8,128)}), f32[6,32,16]{2,0,1:T(8,128)S(1)}, u32[]{:S(2)}, u32[]{:S(2)}) async-start(f32[6,32,16]{2,0,1:T(8,128)} %copy.25), calls=%async_computation.2 | async-start | bytes 262144 | tf_op jit(solution)/shard_map/all_to_all | solution.py:223
  61.2 0.0 copy-done
  61.2 0.7 shard_map.65
  62.0 0.6 broadcast.4
  62.5 1.1 reduce
  63.6 0.9 reshape.28
  64.5 13.6 %all-to-all-done.2 = f32[6,32,16]{2,0,1:T(8,128)S(1)} async-done(((f32[6,32,16]{2,0,1:T(8,128)}), f32[6,32,16]{2,0,1:T(8,128)S(1)}, u32[]{:S(2)}, u32[]{:S(2)}) %all-to-all-start.2) | async-done | bytes 12320 | tf_op jit(solution)/shard_map/all_to_all | solution.py:223
  78.1 14.2 %all-to-all-start.1 = ((bf16[512,2,256]{2,1,0:T(2,128)(2,1)}), bf16[512,2,256]{2,1,0:T(2,128)(2,1)}, u32[]{:S(2)}, u32[]{:S(2)}) async-start(bf16[512,2,256]{2,1,0:T(2,128)(2,1)} %reshape.28), calls=%async_computation.1 | async-start | bytes 1048576 | tf_op jit(solution)/shard_map/all_to_all | solution.py:245
  92.3 0.0 copy-start.5
  92.3 1.2 copy-done.5
  93.5 1.3 shard_map.66
  94.8 0.0 copy-start.3
  94.9 1.0 copy-done.3
  95.8 0.1 reshape.26
  95.9 29.9 %all-to-all-done.1 = bf16[512,2,256]{2,1,0:T(2,128)(2,1)} async-done(((bf16[512,2,256]{2,1,0:T(2,128)(2,1)}), bf16[512,2,256]{2,1,0:T(2,128)(2,1)}, u32[]{:S(2)}, u32[]{:S(2)}) %all-to-all-start.1) | async-done | bytes 524320 | tf_op jit(solution)/shard_map/all_to_all | solution.py:245
  125.9 3.6 %reshape.29 = bf16[512,1,512]{2,1,0:T(2,128)(2,1)S(1)} reshape(bf16[512,2,256]{2,1,0:T(2,128)(2,1)} %all-to-all-done.1) | data formatting | bytes 1048576
  129.4 0.0 copy-start.2
  129.4 0.1 copy.34
  129.6 1.0 copy-done.2
  130.6 0.0 copy-start.4
  130.6 1.2 copy-done.4
  131.8 5.0 %shard_map.67 = bf16[512,512]{1,0:T(8,128)(2,1)S(1)} custom-call(bf16[512,512]{1,0:T(8,128)(2,1)S(1)} %bitcast.11, bf16[2,512,512]{2,1,0:T(8,128)(2,1)S(1)} %get-tuple-element.7.in_prop_ref, bf16[2,512,512]{2,1,0:T(8,128)(2,1)S(1)} %copy-done.4, bf16[6,256,256]{2,1,0:T(8,128)(2,1)S(1)} %copy-done.2, s32[6,16]{1,0:T(8,128)S(1)} %copy.23.pattern_ref, ...), custom_call_target="tpu_custom_call" | custom-call | tf_op jit(solution)/shard_map/pallas_call | solution.py:246
  136.8 1.1 reduce.1
  137.9 0.1 reshape.30
  138.0 43.8 %all_to_all.41 = bf16[512,2,256]{2,1,0:T(2,128)(2,1)S(1)} all-to-all(bf16[512,2,256]{2,1,0:T(2,128)(2,1)S(1)} %reshape.30), channel_id=1, replica_groups=mesh['ra'=16,'rb'=32] {'ra','rb'}, dimensions={0} | all-to-all | bytes 1048576 | tf_op jit(solution)/shard_map/all_to_all | solution.py:252
  181.9 0.4 reshape.31
  182.3 0.1 copy.33
  182.4 0.7 shard_map.68
  183.2 29.9 %all_to_all.42.piece_ref = bf16[16,64,256]{2,1,0:T(8,128)(2,1)S(1)} all-to-all(bf16[16,64,256]{2,1,0:T(8,128)(2,1)S(1)} %shard_map.68), channel_id=1, replica_groups=mesh['ra'=16,'rb'=32] {'ra'}, dimensions={0} | all-to-all | bytes 1048576 | tf_op jit(solution)/shard_map/all_to_all | solution.py:258
  213.1 1.8 shard_map.69
  (3 shorter events, 0.0 us)
Async XLA Ops:
  1.8 1.1 copy-start.1
  2.9 1.0 copy-start.6
  4.0 18.3 %copy-start.7 = (f32[6,32,16]{1,2,0:T(8,128)S(1)}, f32[6,32,16]{1,2,0:T(8,128)}, u32[]{:S(2)}) copy-start(f32[6,32,16]{1,2,0:T(8,128)} %param.9) | copy-start | bytes 36868
  8.1 53.1 %copy-start = (bf16[2,512,512]{2,1,0:T(8,128)(2,1)S(1)}, bf16[2,512,512]{2,1,0:T(8,128)(2,1)}, u32[]{:S(2)}) copy-start(bf16[2,512,512]{2,1,0:T(8,128)(2,1)} %prop_ref.5) | copy-start | bytes 3145732
  8.1 40.3 %all-to-all-start = ((bf16[16,64,256]{2,1,0:T(8,128)(2,1)}), bf16[16,64,256]{2,1,0:T(8,128)(2,1)S(1)}, u32[]{:S(2)}, u32[]{:S(2)}) async-start(bf16[16,64,256]{2,1,0:T(8,128)(2,1)} %shard_map.64), calls=%async_computation | async-start | bytes 1048576 | tf_op jit(solution)/shard_map/all_to_all | solution.py:239
  48.4 29.7 %all-to-all-start.2 = ((f32[6,32,16]{2,0,1:T(8,128)}), f32[6,32,16]{2,0,1:T(8,128)S(1)}, u32[]{:S(2)}, u32[]{:S(2)}) async-start(f32[6,32,16]{2,0,1:T(8,128)} %copy.25), calls=%async_computation.2 | async-start | bytes 262144 | tf_op jit(solution)/shard_map/all_to_all | solution.py:223
  78.1 47.7 %all-to-all-start.1 = ((bf16[512,2,256]{2,1,0:T(2,128)(2,1)}), bf16[512,2,256]{2,1,0:T(2,128)(2,1)}, u32[]{:S(2)}, u32[]{:S(2)}) async-start(bf16[512,2,256]{2,1,0:T(2,128)(2,1)} %reshape.28), calls=%async_computation.1 | async-start | bytes 1048576 | tf_op jit(solution)/shard_map/all_to_all | solution.py:245
  92.3 1.2 copy-start.5
  94.8 1.0 copy-start.3
  129.4 1.1 copy-start.2
  130.6 1.2 copy-start.4

commit v2 on v1

--- a/solution.py
+++ b/solution.py
@@ -220,8 +220,11 @@
 
     pad = (-terms) % 8
     here = jnp.pad(radial.reshape(terms, cells), ((0, pad), (0, 0)))
-    there = lax.all_to_all(radial, "rb", split_axis=1, concat_axis=2, tiled=True)
-    there = jnp.pad(there.reshape(terms, r2), ((0, pad), (0, 0)))
+    packed = radial.transpose(1, 0, 2).reshape(rows * terms * cols // LANES, LANES)
+    everyone = lax.all_gather(jnp.pad(packed, ((0, 64 - packed.shape[0]), (0, 0))), "rb", axis=0, tiled=False)
+    mine = everyone[:, :packed.shape[0]].reshape(peers, rows, terms, cols)
+    mine = lax.dynamic_index_in_dim(mine, lax.axis_index("rb"), 1, keepdims=False)
+    there = jnp.pad(mine.transpose(1, 0, 2).reshape(terms, r2), ((0, pad), (0, 0)))
 
     piece = call(
         functools.partial(first_kick_kernel, groups, cols),

time: 216 us -> 253 us (1.17)
  waiting for transfers between devices: 68.9 us -> 94.2 us
  between operations: 0.17 us -> 13.6 us
  starting transfers between devices: 41.1 us -> 33.1 us
  local copies, waits for them, and re-layouts: 15.1 us -> 19.5 us
    all_gather x0 -> x1, waiting for transfers between devices: none -> 68.9 us  [on_device(): lax.all_gather(jnp.pad(packed, ((0, 64 - packed.shape[0]), (0, 0))), 'rb'...]
    all_to_all x1, waiting for transfers between devices: 29.9 us -> 0.01 us  [on_device(): lax.all_to_all(half, ('ra', 'rb'), split_axis=0, concat_axis=0, tiled=True)]
    all_to_all x1 -> x0, waiting for transfers between devices: 13.6 us -> none  [on_device(): lax.all_to_all(radial, 'rb', split_axis=1, concat_axis=2, tiled=True)]
    all_to_all x1 -> x0, starting transfers between devices: 12.8 us -> none  [on_device(): lax.all_to_all(radial, 'rb', split_axis=1, concat_axis=2, tiled=True)]
    all_to_all x1, starting transfers between devices: 14.2 us -> 19 us  [on_device(): lax.all_to_all(half, ('ra', 'rb'), split_axis=0, concat_axis=0, tiled=True)]
  transfers between devices with their start and end apart: 3 -> 3, of which waited for: 3 -> 2; matrix products, arithmetic and copies ran while one was open for 2% -> 3% of each run, Pallas kernels for 1% -> 1%
where the time goes in v2:
time: 253 us; the launch traced here: 252 us
  waiting for transfers between devices  94.2 us (37%)
  blocking collectives  76.3 us (30%)
  starting transfers between devices  33.1 us (13%)
  local copies, waits for them, and re-layouts  19.5 us (8%)
  Pallas kernels  13.7 us (5%)
  between operations  13.6 us (5%)
    all_gather x1, waiting for transfers between devices, on_device(): lax.all_gather(jnp.pad(packed, ((0, 64 - packed.shape[0]), (0, 0))), 'rb'...  68.9 us
    all_to_all x1, blocking collectives, on_device(): lax.all_to_all(half, ('ra', 'rb'), split_axis=0, concat_axis=0, tiled=True)  46.3 us
    all_to_all x1, blocking collectives, on_device(): piece = lax.all_to_all(piece, 'ra', split_axis=0, concat_axis=0, tiled=True)  29.9 us
    all_to_all x1, waiting for transfers between devices, on_device(): piece = lax.all_to_all(piece, 'ra', split_axis=0, concat_axis=0, tiled=True)  25.3 us
    all_to_all x1, starting transfers between devices, on_device(): lax.all_to_all(half, ('ra', 'rb'), split_axis=0, concat_axis=0, tiled=True)  19 us
    unnamed x24, local copies, waits for them, and re-layouts  14.5 us
    all_to_all x1, starting transfers between devices, on_device(): piece = lax.all_to_all(piece, 'ra', split_axis=0, concat_axis=0, tiled=True)  14 us
  transfers between devices with their start and end apart: 3, of which 2 were waited for; matrix products, arithmetic and copies ran while one was open for 3% of the time, Pallas kernels for 1%

profile of v2, /device:TPU:1, one launch (start us, length us, event | category | flops | bytes accessed | tf_op | source)
XLA Modules:
  0.0 252.3 jit_solution(16085787745395642370)
XLA Ops:
  6.5 0.8 copy.30.pattern_ref
  7.3 0.0 copy-start.7
  7.3 0.9 copy.29
  8.3 0.1 reshape.27
  8.4 0.0 copy-start.1
  8.4 1.1 copy-done.1
  9.5 1.0 copy-done.6
  10.6 4.1 %shard_map.64 = bf16[16,64,256]{2,1,0:T(8,128)(2,1)} custom-call(bf16[1024,256]{1,0:T(8,128)(2,1)S(1)} %bitcast.22, bf16[6,256,256]{2,1,0:T(8,128)(2,1)S(1)} %copy-done.1, s32[6,16]{1,0:T(8,128)S(1)} %copy.30.pattern_ref, f32[8,512]{1,0:T(8,128)S(1)} %pad.11.radial_ref), custom_call_target="tpu_custom_call" | custom-call | tf_op jit(solution)/shard_map/pallas_call | solution.py:229
  14.7 14.0 %all-to-all-start = ((bf16[16,64,256]{2,1,0:T(8,128)(2,1)}), bf16[16,64,256]{2,1,0:T(8,128)(2,1)S(1)}, u32[]{:S(2)}, u32[]{:S(2)}) async-start(bf16[16,64,256]{2,1,0:T(8,128)(2,1)} %shard_map.64), calls=%async_computation | async-start | bytes 1048576 | tf_op jit(solution)/shard_map/all_to_all | solution.py:242
  28.7 0.0 all-gather.3.cloned.1.call-start
  28.8 0.0 copy-done.7
  28.8 0.1 copy.32
  28.9 0.1 reshape.28
  29.0 0.6 pad.12
  29.6 0.0 all-gather.3.cloned.1.call-update
  29.6 25.3 %all-to-all-done.piece_ref = bf16[16,64,256]{2,1,0:T(8,128)(2,1)S(1)} async-done(((bf16[16,64,256]{2,1,0:T(8,128)(2,1)}), bf16[16,64,256]{2,1,0:T(8,128)(2,1)S(1)}, u32[]{:S(2)}, u32[]{:S(2)}) %all-to-all-start) | async-done | bytes 524320 | tf_op jit(solution)/shard_map/all_to_all | solution.py:242
  54.9 0.0 copy-done
  54.9 0.7 shard_map.65
  55.6 0.5 broadcast.6
  56.1 1.0 reduce
  57.1 0.9 reshape.33
  58.0 19.0 %all-to-all-start.1 = ((bf16[512,2,256]{2,1,0:T(2,128)(2,1)}), bf16[512,2,256]{2,1,0:T(2,128)(2,1)}, u32[]{:S(2)}, u32[]{:S(2)}) async-start(bf16[512,2,256]{2,1,0:T(2,128)(2,1)} %reshape.33), calls=%async_computation.1 | async-start | bytes 1048576 | tf_op jit(solution)/shard_map/all_to_all | solution.py:248
  77.0 0.0 copy-start.5
  77.0 1.2 copy-done.5
  78.3 1.3 shard_map.66
  79.6 0.0 copy-start.3
  79.6 68.9 %all-gather.3.cloned.1.call-done = f32[2048,128]{1,0:T(8,128)} async-done(((f32[64,128]{1,0:T(8,128)}), f32[2048,128]{1,0:T(8,128)}) %all-gather.3.cloned.1.call-update) | async-done | bytes 1048592 | tf_op jit(solution)/shard_map/all_gather | solution.py:224
  148.5 1.8 slice.4
  150.3 2.6 %copy.39 = f32[32,24,128]{0,2,1:T(8,128)} copy(f32[32,24,128]{2,1,0:T(8,128)} %slice.4) | data formatting | bytes 786432
  152.9 0.8 dynamic-slice_bitcast_fusion
  153.7 0.1 copy.34
  153.8 0.1 reshape.30
  153.9 0.0 copy-done.3
  153.9 0.0 copy-start.2
  153.9 0.0 all-to-all-done.1
  153.9 4.4 %reshape.34 = bf16[512,1,512]{2,1,0:T(2,128)(2,1)} reshape(bf16[512,2,256]{2,1,0:T(2,128)(2,1)} %all-to-all-done.1) | data formatting | bytes 1048576
  158.4 1.4 copy.43
  159.8 0.0 copy-done.2
  159.8 0.1 copy-done.4
  159.9 5.0 %shard_map.67 = bf16[512,512]{1,0:T(8,128)(2,1)S(1)} custom-call(bf16[512,512]{1,0:T(8,128)(2,1)S(1)} %bitcast.18, bf16[2,512,512]{2,1,0:T(8,128)(2,1)S(1)} %get-tuple-element.7.in_prop_ref, bf16[2,512,512]{2,1,0:T(8,128)(2,1)S(1)} %copy-done.4, bf16[6,256,256]{2,1,0:T(8,128)(2,1)S(1)} %copy-done.2, s32[6,16]{1,0:T(8,128)S(1)} %copy.30.pattern_ref, ...), custom_call_target="tpu_custom_call" | custom-call | tf_op jit(solution)/shard_map/pallas_call | solution.py:249
  164.9 1.0 reduce.1
  165.9 0.1 reshape.35
  166.1 46.3 %all_to_all.32 = bf16[512,2,256]{2,1,0:T(2,128)(2,1)S(1)} all-to-all(bf16[512,2,256]{2,1,0:T(2,128)(2,1)S(1)} %reshape.35), channel_id=1, replica_groups=mesh['ra'=16,'rb'=32] {'ra','rb'}, dimensions={0} | all-to-all | bytes 1048576 | tf_op jit(solution)/shard_map/all_to_all | solution.py:255
  212.4 0.4 reshape.36
  212.9 0.1 copy.42
  213.0 0.7 shard_map.68
  213.7 29.9 %all_to_all.33.piece_ref = bf16[16,64,256]{2,1,0:T(8,128)(2,1)S(1)} all-to-all(bf16[16,64,256]{2,1,0:T(8,128)(2,1)S(1)} %shard_map.68), channel_id=1, replica_groups=mesh['ra'=16,'rb'=32] {'ra'}, dimensions={0} | all-to-all | bytes 1048576 | tf_op jit(solution)/shard_map/all_to_all | solution.py:261
  243.7 1.8 shard_map.69
  (5 shorter events, 0.0 us)
Async XLA Ops:
  7.3 21.5 %copy-start.7 = (f32[6,32,16]{1,2,0:T(8,128)S(1)}, f32[6,32,16]{1,2,0:T(8,128)}, u32[]{:S(2)}) copy-start(f32[6,32,16]{1,2,0:T(8,128)} %param.9) | copy-start | bytes 36868
  8.4 1.1 copy-start.1
  9.5 1.0 copy-start.6
  10.6 44.3 %copy-start = (bf16[2,512,512]{2,1,0:T(8,128)(2,1)S(1)}, bf16[2,512,512]{2,1,0:T(8,128)(2,1)}, u32[]{:S(2)}) copy-start(bf16[2,512,512]{2,1,0:T(8,128)(2,1)} %prop_ref.5) | copy-start | bytes 3145732
  14.7 40.2 %all-to-all-start = ((bf16[16,64,256]{2,1,0:T(8,128)(2,1)}), bf16[16,64,256]{2,1,0:T(8,128)(2,1)S(1)}, u32[]{:S(2)}, u32[]{:S(2)}) async-start(bf16[16,64,256]{2,1,0:T(8,128)(2,1)} %shard_map.64), calls=%async_computation | async-start | bytes 1048576 | tf_op jit(solution)/shard_map/all_to_all | solution.py:242
  28.7 119.8 %all-gather.3.cloned.1.call-start = ((), (), s32[]{:S(2)}) async-start(), calls=%async_computation.4 | async-start | bytes 1081344 | tf_op jit(solution)/shard_map/all_gather | solution.py:224
  58.0 95.9 %all-to-all-start.1 = ((bf16[512,2,256]{2,1,0:T(2,128)(2,1)}), bf16[512,2,256]{2,1,0:T(2,128)(2,1)}, u32[]{:S(2)}, u32[]{:S(2)}) async-start(bf16[512,2,256]{2,1,0:T(2,128)(2,1)} %reshape.33), calls=%async_computation.1 | async-start | bytes 1048576 | tf_op jit(solution)/shard_map/all_to_all | solution.py:248
  77.0 1.2 copy-start.5
  79.6 74.3 %copy-start.3 = (bf16[2,512,512]{2,1,0:T(8,128)(2,1)}, bf16[2,512,512]{2,1,0:T(8,128)(2,1)S(1)}, u32[]{:S(2)}) copy-start(bf16[2,512,512]{2,1,0:T(8,128)(2,1)S(1)} %get-tuple-element.8.out_prop_ref) | copy-start | bytes 3145732
  153.9 5.9 %copy-start.2 = (bf16[6,256,256]{2,1,0:T(8,128)(2,1)S(1)}, bf16[6,256,256]{2,1,0:T(8,128)(2,1)}, u32[]{:S(2)}) copy-start(bf16[6,256,256]{2,1,0:T(8,128)(2,1)} %coupling_ref.3) | copy-start | bytes 2359300
  158.4 1.5 copy-start.4
Sparse Core Ops, SparseCore 0:
  33.8 114.5 all-gather.2

commit v3 on v1

--- a/solution.py
+++ b/solution.py
@@ -55,49 +55,75 @@
         mask = jnp.zeros((block, channels), F32)
         for j in range(count):
             inside = (lane >= j * block) & (lane < (j + 1) * block)
-            mask = jnp.where(inside, pattern_ref[term, i * count + j].astype(F32), mask)
+            mask = jnp.where(inside, pattern_ref[term, i, j].astype(F32), mask)
         piece = coupling_ref[term, i * block:(i + 1) * block, :].astype(F32) * mask
         rows.append(piece.astype(BF16))
     return jnp.concatenate(rows, axis=0)
 
 
-def kick_into(real, imag, coupling_ref, pattern_ref, factors, block, store):
-    terms = coupling_ref.shape[0]
-    weights = [masked_weights(coupling_ref, pattern_ref, k, block) for k in range(terms)]
-    rows = real.shape[0]
-    step = 128
-    for start in range(0, rows, step):
-        re = real[start:start + step, :]
-        im = imag[start:start + step, :]
+def kick_into(load, weights, factor_of, rows, count, store):
+    together = max(1, 128 // rows)
+    for first in range(0, count, together):
+        blocks = range(first, first + together)
+        re, im = load(first * rows, together * rows)
         sum_re = jnp.zeros(re.shape, F32)
         sum_im = jnp.zeros(re.shape, F32)
-        for k in range(terms):
-            factor = factors[start:start + step, k:k + 1]
+        for k in range(len(weights)):
+            factor = jnp.concatenate([factor_of(k, n) for n in blocks], axis=0)
             sum_re = sum_re + dot_rows(re, weights[k]) * factor
             sum_im = sum_im + dot_rows(im, weights[k]) * factor
-        store(start, step, re.astype(F32) + sum_im, im.astype(F32) - sum_re)
-
-
-def first_kick_kernel(groups, cols, amp_ref, coupling_ref, pattern_ref, radial_ref, out_ref, held):
-    cells = amp_ref.shape[0] // 2
-    channels = amp_ref.shape[1]
-    block = channels // 4
-    factors = radial_ref[...].T
-
-    def store(start, step, re, im):
-        for h in range(channels // LANES):
-            held[h, start:start + step, :] = re[:, h * LANES:(h + 1) * LANES]
-            held[h, cells + start:cells + start + step, :] = im[:, h * LANES:(h + 1) * LANES]
-
-    kick_into(amp_ref[:cells, :], amp_ref[cells:, :], coupling_ref, pattern_ref, factors, block, store)
-    width = channels // groups
-    rows = cells // cols
+        store(first * rows, re.astype(F32) + sum_im, im.astype(F32) - sum_re)
+
+
+def order(prop_ref, out_ref, inner):
+    size = prop_ref.shape[1]
+    outer = size // inner
+    row = lax.broadcasted_iota(jnp.int32, (size, size), 0)
+    col = lax.broadcasted_iota(jnp.int32, (size, size), 1)
+    place = (row % outer) * inner + row // outer
+    move = jnp.where(col == place, 1.0, 0.0).astype(BF16)
+    for part in range(2):
+        out_ref[part] = dot(move, dot_rows(prop_ref[part], move).astype(BF16)).astype(BF16)
+
+
+def halves_of(value):
+    return [value[:, h * LANES:(h + 1) * LANES] for h in range(value.shape[1] // LANES)]
+
+
+def first_kick_kernel(groups, amp_ref, coupling_ref, pattern_ref, radial_ref, prop_ref,
+                      out_ref, weights_ref, ordered_ref, held, moved, kicked):
+    terms, rows, cols = radial_ref.shape
+    cells = rows * cols
+    channels = coupling_ref.shape[1]
+    block = channels // pattern_ref.shape[1]
+    parts = channels // LANES
+    weights = [masked_weights(coupling_ref, pattern_ref, k, block) for k in range(terms)]
+    for k in range(terms):
+        weights_ref[k] = weights[k]
+    order(prop_ref, ordered_ref, cols)
+    for h in range(parts):
+        held[h] = amp_ref[:, h * LANES:(h + 1) * LANES].astype(F32)
+    for part in range(2):
+        for b in range(cols):
+            place = pl.ds(part * cells + b, rows, stride=cols)
+            moved[part, b * rows:(b + 1) * rows, :] = jnp.concatenate(
+                [held[h, place, :] for h in range(parts)], axis=1
+            ).astype(BF16)
+
+    def load(start, size):
+        return moved[0, start:start + size, :], moved[1, start:start + size, :]
+
+    def store(start, re, im):
+        kicked[0, start:start + re.shape[0], :] = re
+        kicked[1, start:start + im.shape[0], :] = im
+
+    kick_into(load, weights, lambda k, b: radial_ref[k, :, b:b + 1], rows, cols, store)
+    width = channels // groups
     for part in range(2):
         for a in range(0, rows, 16):
-            tiles = []
-            for b in range(cols):
-                place = pl.ds(part * cells + a * cols + b, 16, stride=cols)
-                tiles.append([held[h, place, :] for h in range(channels // LANES)])
+            tiles = [
+                halves_of(kicked[part, b * rows + a:b * rows + a + 16, :]) for b in range(cols)
+            ]
             tiles = swap_blocks(tiles, width)
             for g in range(groups):
                 out_ref[g, part * rows + a:part * rows + a + 16, :] = jnp.concatenate(
@@ -127,21 +153,8 @@
     out_ref[:, rows:, :] = im.astype(BF16).reshape(groups, rows, lanes)
 
 
-def order_kernel(outer, inner, prop_ref, in_ref, out_ref):
-    size = prop_ref.shape[1]
-    row = lax.broadcasted_iota(jnp.int32, (size, size), 0)
-    col = lax.broadcasted_iota(jnp.int32, (size, size), 1)
-    place = (row % outer) * inner + row // outer
-    move = jnp.where(col == place, 1.0, 0.0).astype(BF16)
-    for part in range(2):
-        in_ref[part] = dot_rows(prop_ref[part], move).astype(BF16)
-        out_ref[part] = dot(move, prop_ref[part]).astype(BF16)
-
-
-def second_kernel(groups, cols, piece_ref, in_prop_ref, out_prop_ref, coupling_ref, pattern_ref,
-                  radial_ref, out_ref, state, kicked):
-    channels = coupling_ref.shape[1]
-    block = channels // 4
+def second_kernel(groups, cols, piece_ref, prop_ref, weights_ref, radial_ref, out_ref, state, kicked):
+    terms, channels = weights_ref.shape[0], weights_ref.shape[1]
     width = channels // groups
     peers = piece_ref.shape[0] // groups
     lanes = cols * width
@@ -158,15 +171,22 @@
                 state[part, b * peers + s:b * peers + s + 16, :] = jnp.concatenate(
                     tiles[b], axis=1
                 ).astype(BF16)
-    re, im = complex_dot(in_prop_ref[0], in_prop_ref[1], state[0], state[1])
-    factors = radial_ref[...].T
-
-    def store(start, step, new_re, new_im):
-        kicked[0, start:start + step, :] = new_re.astype(BF16)
-        kicked[1, start:start + step, :] = new_im.astype(BF16)
-
-    kick_into(re.astype(BF16), im.astype(BF16), coupling_ref, pattern_ref, factors, block, store)
-    re, im = complex_dot(out_prop_ref[0], out_prop_ref[1], kicked[0], kicked[1])
+    re, im = complex_dot(prop_ref[0], prop_ref[1], state[0], state[1])
+    state[0] = re.astype(BF16)
+    state[1] = im.astype(BF16)
+
+    def load(start, size):
+        return state[0, start:start + size, :], state[1, start:start + size, :]
+
+    def store(start, new_re, new_im):
+        kicked[0, start:start + new_re.shape[0], :] = new_re.astype(BF16)
+        kicked[1, start:start + new_im.shape[0], :] = new_im.astype(BF16)
+
+    weights = [weights_ref[k] for k in range(terms)]
+    kick_into(
+        load, weights, lambda k, b: radial_ref[:, k * cols + b:k * cols + b + 1], peers, cols, store
+    )
+    re, im = complex_dot(prop_ref[0], prop_ref[1], kicked[0], kicked[1])
     state[0] = re.astype(BF16)
     state[1] = im.astype(BF16)
     for part in range(2):
@@ -206,7 +226,7 @@
 def on_device(amplitude, coupling, pattern, radial, first_prop, second_prop):
     _, rows, cols, channels = amplitude.shape
     cells = rows * cols
-    terms, count = pattern.shape[0], pattern.shape[1]
+    terms = pattern.shape[0]
     groups, peers = lax.axis_size("ra"), lax.axis_size("rb")
     width = channels // groups
     lanes = cols * width
@@ -216,26 +236,28 @@
     smem = pl.BlockSpec(memory_space=pltpu.SMEM)
     call = functools.partial(pl.pallas_call, compiler_params=params, out_specs=vmem)
     shape = jax.ShapeDtypeStruct
-    flat_pattern = pattern.reshape(terms, count * count)
-
-    pad = (-terms) % 8
-    here = jnp.pad(radial.reshape(terms, cells), ((0, pad), (0, 0)))
-    there = lax.all_to_all(radial, "rb", split_axis=1, concat_axis=2, tiled=True)
-    there = jnp.pad(there.reshape(terms, r2), ((0, pad), (0, 0)))
-
-    piece = call(
-        functools.partial(first_kick_kernel, groups, cols),
-        out_shape=shape((groups, 2 * rows, lanes), BF16),
-        in_specs=[vmem, vmem, smem, vmem],
-        scratch_shapes=[pltpu.VMEM((channels // LANES, 2 * cells, LANES), F32)],
-    )(amplitude.reshape(2 * cells, channels), coupling, flat_pattern, here)
-    ordered = pl.pallas_call(
-        functools.partial(order_kernel, peers, cols),
-        out_shape=[shape((2, r2, r2), BF16)] * 2,
-        in_specs=[vmem],
-        out_specs=[vmem, vmem],
+
+    packed = radial.transpose(1, 0, 2).reshape(rows, terms * cols)
+    packed = jnp.pad(packed, ((0, 0), (0, (-terms * cols) % LANES)))
+    packed = lax.all_to_all(packed, "rb", split_axis=0, concat_axis=0, tiled=True)
+
+    piece, weights, ordered = pl.pallas_call(
+        functools.partial(first_kick_kernel, groups),
+        out_shape=[
+            shape((groups, 2 * rows, lanes), BF16),
+            shape(coupling.shape, BF16),
+            shape(second_prop.shape, BF16),
+        ],
+        in_specs=[vmem, vmem, smem, vmem, vmem],
+        out_specs=[vmem] * 3,
+        scratch_shapes=[
+            pltpu.VMEM((channels // LANES, 2 * cells, LANES), F32),
+            pltpu.VMEM((2, cells, channels), BF16),
+            pltpu.VMEM((2, cells, channels), F32),
+        ],
         compiler_params=params,
-    )(second_prop)
+    )(amplitude.reshape(2 * cells, channels), coupling, pattern, radial, second_prop)
+    piece, packed = lax.optimization_barrier((piece, packed))
     piece = lax.all_to_all(piece, "ra", split_axis=0, concat_axis=0, tiled=True)
     half = call(
         first_forward_kernel,
@@ -246,9 +268,9 @@
     half = call(
         functools.partial(second_kernel, groups, cols),
         out_shape=shape((groups * peers, 2 * lanes), BF16),
-        in_specs=[vmem, vmem, vmem, vmem, smem, vmem],
+        in_specs=[vmem] * 4,
         scratch_shapes=[pltpu.VMEM((2, r2, channels), BF16)] * 2,
-    )(half, *ordered, coupling, flat_pattern, there)
+    )(half, ordered, weights, packed)
     half = lax.all_to_all(half, ("ra", "rb"), split_axis=0, concat_axis=0, tiled=True)
     piece = call(
         first_back_kernel,

time: 216 us -> 210 us (0.972)
  blocking collectives: 73.8 us -> 155 us
  waiting for transfers between devices: 68.9 us -> 6.79 us
  starting transfers between devices: 41.1 us -> 21.1 us
  local copies, waits for them, and re-layouts: 15.1 us -> 11.8 us
    all_to_all x3 -> x1, waiting for transfers between devices: 68.9 us -> 6.79 us  [on_device(): lax.all_to_all(packed, 'rb', split_axis=0, concat_axis=0, tiled=True)]
    all_to_all x1 -> x2, blocking collectives: 43.8 us -> 91.9 us  [on_device(): lax.all_to_all(half, ('ra', 'rb'), split_axis=0, concat_axis=0, tiled=True)]
    all_to_all x1 -> x2, blocking collectives: 29.9 us -> 63 us  [on_device(): piece = lax.all_to_all(piece, 'ra', split_axis=0, concat_axis=0, tiled=True)]
    all_to_all x3 -> x1, starting transfers between devices: 41.1 us -> 21.1 us  [on_device(): lax.all_to_all(packed, 'rb', split_axis=0, concat_axis=0, tiled=True)]
    unnamed x24 -> x20, local copies, waits for them, and re-layouts: 13.5 us -> 9.87 us
    pallas_call x2 -> x1, Pallas kernels: 5.45 us -> 4.69 us  [on_device(): pl.pallas_call(functools.partial(first_kick_kernel, groups), out_shape=[s...]
  transfers between devices with their start and end apart: 3 -> 1, of which waited for: 3 -> 1; matrix products, arithmetic and copies ran while one was open for 2% -> 0% of each run, Pallas kernels for 1% -> 2%
where the time goes in v3:
time: 210 us
  blocking collectives  155 us (74%)
  starting transfers between devices  21.1 us (10%)
  Pallas kernels  12.3 us (6%)
  local copies, waits for them, and re-layouts  11.8 us (6%)
  waiting for transfers between devices  6.79 us (3%)
  other arithmetic  2.53 us (1%)
    all_to_all x2, blocking collectives, on_device(): lax.all_to_all(half, ('ra', 'rb'), split_axis=0, concat_axis=0, tiled=True)  91.9 us
    all_to_all x2, blocking collectives, on_device(): piece = lax.all_to_all(piece, 'ra', split_axis=0, concat_axis=0, tiled=True)  63 us
    all_to_all x1, starting transfers between devices, on_device(): lax.all_to_all(packed, 'rb', split_axis=0, concat_axis=0, tiled=True)  21.1 us
    unnamed x20, local copies, waits for them, and re-layouts  9.87 us
    all_to_all x1, waiting for transfers between devices, on_device(): lax.all_to_all(packed, 'rb', split_axis=0, concat_axis=0, tiled=True)  6.79 us
    pallas_call x1, Pallas kernels, on_device(): pl.pallas_call(functools.partial(first_kick_kernel, groups), out_shape=[s...  4.69 us
    pallas_call x1, Pallas kernels, on_device(): call(functools.partial(second_kernel, groups, cols), out_shape=shape((gro...  4.35 us
  transfers between devices with their start and end apart: 1, of which 1 were waited for; matrix products, arithmetic and copies ran while one was open for 0% of the time, Pallas kernels for 2%

profile of v3, /device:TPU:1, one launch (start us, length us, event | category | flops | bytes accessed | tf_op | source)
XLA Modules:
  0.0 209.6 jit_solution(6805057841510479597)
XLA Ops:
  0.0 0.8 pad_bitcast_fusion
  0.8 0.0 copy-start.4
  0.8 0.7 copy.20
  1.5 21.1 %all-to-all-start = ((f32[32,1,128]{2,1,0:T(1,128)}), f32[32,1,128]{2,1,0:T(1,128)S(1)}, u32[]{:S(2)}, u32[]{:S(2)}) async-start(f32[32,1,128]{2,1,0:T(1,128)} %copy.20), calls=%async_computation | async-start | bytes 32768 | tf_op jit(solution)/shard_map/all_to_all | solution.py:242
  22.6 0.0 copy-done.4
  22.6 0.0 copy-start.5
  22.6 0.1 copy.19.radial_ref
  22.7 0.6 copy-done.5
  23.3 0.1 copy.18.pattern_ref
  23.4 0.0 copy-start.1
  23.4 1.2 copy-done.1
  24.7 0.0 copy-start.2
  24.7 1.1 copy-done.2
  25.8 0.0 copy-start.3
  25.8 1.0 copy-done.3
  26.8 4.7 %shard_map.64 = (bf16[16,64,256]{2,1,0:T(8,128)(2,1)S(1)}, bf16[6,256,256]{2,1,0:T(8,128)(2,1)S(1)}, bf16[2,512,512]{2,1,0:T(8,128)(2,1)S(1)}) custom-call(bf16[1024,256]{1,0:T(8,128)(2,1)S(1)} %bitcast.20, bf16[6,256,256]{2,1,0:T(8,128)(2,1)S(1)} %copy-done.2, s32[6,4,4]{2,1,0:T(4,128)S(1)} %copy.18.pattern_ref, f32[6,32,16]{2,1,0:T(8,128)S(1)} %copy.19.radial_ref, ...), custom_call_target="tpu_custom_call" | custom-call | tf_op jit(solution)/shard_map/pallas_call | solution.py:244
  31.5 0.0 copy-start
  31.5 6.8 %all-to-all-done = f32[32,1,128]{2,1,0:T(1,128)S(1)} async-done(((f32[32,1,128]{2,1,0:T(1,128)}), f32[32,1,128]{2,1,0:T(1,128)S(1)}, u32[]{:S(2)}, u32[]{:S(2)}) %all-to-all-start) | async-done | bytes 16416 | tf_op jit(solution)/shard_map/all_to_all | solution.py:242
  38.3 33.1 %all_to_all.44.piece_ref = bf16[16,64,256]{2,1,0:T(8,128)(2,1)S(1)} all-to-all(bf16[16,64,256]{2,1,0:T(8,128)(2,1)S(1)} %get-tuple-element.11), channel_id=1, replica_groups=mesh['ra'=16,'rb'=32] {'ra'}, dimensions={0} | all-to-all | bytes 1048576 | tf_op jit(solution)/shard_map/all_to_all | solution.py:261
  71.4 0.0 copy-done
  71.4 0.7 shard_map.65
  72.1 0.5 broadcast.2
  72.6 1.6 reduce
  74.2 2.0 reshape.18
  76.2 47.7 %all_to_all.45 = bf16[512,2,256]{2,1,0:T(2,128)(2,1)S(1)} all-to-all(bf16[512,2,256]{2,1,0:T(2,128)(2,1)} %reshape.18), channel_id=1, replica_groups=mesh['ra'=16,'rb'=32] {'ra','rb'}, dimensions={0} | all-to-all | bytes 1048576 | tf_op jit(solution)/shard_map/all_to_all | solution.py:267
  123.9 1.7 reshape.19
  125.5 1.3 copy.28
  126.9 4.4 %shard_map.66 = bf16[512,512]{1,0:T(8,128)(2,1)S(1)} custom-call(bf16[512,512]{1,0:T(8,128)(2,1)S(1)} %bitcast.16, bf16[2,512,512]{2,1,0:T(8,128)(2,1)S(1)} %get-tuple-element.12.prop_ref, bf16[6,256,256]{2,1,0:T(8,128)(2,1)S(1)} %get-tuple-element.13.weights_ref, f32[32,128]{1,0:T(8,128)S(1)} %bitcast.21), custom_call_target="tpu_custom_call" | custom-call | tf_op jit(solution)/shard_map/pallas_call | solution.py:268
  131.3 1.0 reduce.1
  132.2 0.1 reshape.20
  132.3 44.2 %all_to_all.46 = bf16[512,2,256]{2,1,0:T(2,128)(2,1)S(1)} all-to-all(bf16[512,2,256]{2,1,0:T(2,128)(2,1)S(1)} %reshape.20), channel_id=1, replica_groups=mesh['ra'=16,'rb'=32] {'ra','rb'}, dimensions={0} | all-to-all | bytes 1048576 | tf_op jit(solution)/shard_map/all_to_all | solution.py:274
  176.5 0.4 reshape.21
  176.9 0.1 copy.27
  177.1 0.7 shard_map.67
  177.8 29.9 %all_to_all.47.piece_ref = bf16[16,64,256]{2,1,0:T(8,128)(2,1)S(1)} all-to-all(bf16[16,64,256]{2,1,0:T(8,128)(2,1)S(1)} %shard_map.67), channel_id=1, replica_groups=mesh['ra'=16,'rb'=32] {'ra'}, dimensions={0} | all-to-all | bytes 1048576 | tf_op jit(solution)/shard_map/all_to_all | solution.py:280
  207.7 1.8 shard_map.68
Async XLA Ops:
  0.8 21.8 %copy-start.4 = (f32[6,32,16]{1,2,0:T(8,128)S(1)}, f32[6,32,16]{1,2,0:T(8,128)}, u32[]{:S(2)}) copy-start(f32[6,32,16]{1,2,0:T(8,128)} %param.9) | copy-start | bytes 36868
  1.5 36.9 %all-to-all-start = ((f32[32,1,128]{2,1,0:T(1,128)}), f32[32,1,128]{2,1,0:T(1,128)S(1)}, u32[]{:S(2)}, u32[]{:S(2)}) async-start(f32[32,1,128]{2,1,0:T(1,128)} %copy.20), calls=%async_computation | async-start | bytes 32768 | tf_op jit(solution)/shard_map/all_to_all | solution.py:242
  22.6 0.7 copy-start.5
  23.4 1.2 copy-start.1
  24.7 1.1 copy-start.2
  25.8 1.0 copy-start.3
  31.5 39.9 %copy-start = (bf16[2,512,512]{2,1,0:T(8,128)(2,1)S(1)}, bf16[2,512,512]{2,1,0:T(8,128)(2,1)}, u32[]{:S(2)}) copy-start(bf16[2,512,512]{2,1,0:T(8,128)(2,1)} %prop_ref.5) | copy-start | bytes 3145732

commit v4 on v3

--- a/solution.py
+++ b/solution.py
@@ -90,17 +90,19 @@
     return [value[:, h * LANES:(h + 1) * LANES] for h in range(value.shape[1] // LANES)]
 
 
-def first_kick_kernel(groups, amp_ref, coupling_ref, pattern_ref, radial_ref, prop_ref,
-                      out_ref, weights_ref, ordered_ref, held, moved, kicked):
+def tables_kernel(inner, coupling_ref, pattern_ref, prop_ref, weights_ref, ordered_ref):
+    block = coupling_ref.shape[1] // pattern_ref.shape[1]
+    for k in range(coupling_ref.shape[0]):
+        weights_ref[k] = masked_weights(coupling_ref, pattern_ref, k, block)
+    order(prop_ref, ordered_ref, inner)
+
+
+def first_kick_kernel(groups, amp_ref, weights_ref, radial_ref, out_ref, held, moved, kicked):
     terms, rows, cols = radial_ref.shape
     cells = rows * cols
-    channels = coupling_ref.shape[1]
-    block = channels // pattern_ref.shape[1]
+    channels = weights_ref.shape[1]
     parts = channels // LANES
-    weights = [masked_weights(coupling_ref, pattern_ref, k, block) for k in range(terms)]
-    for k in range(terms):
-        weights_ref[k] = weights[k]
-    order(prop_ref, ordered_ref, cols)
+    weights = [weights_ref[k] for k in range(terms)]
     for h in range(parts):
         held[h] = amp_ref[:, h * LANES:(h + 1) * LANES].astype(F32)
     for part in range(2):
@@ -141,14 +143,14 @@
     k_re = piece_ref[:, :rows, :].reshape(groups * rows, lanes)
     k_im = piece_ref[:, rows:, :].reshape(groups * rows, lanes)
     re, im = complex_dot(prop_ref[0], prop_ref[1], k_re, k_im)
-    out_ref[:, :lanes] = re.astype(BF16)
-    out_ref[:, lanes:] = im.astype(BF16)
+    out_ref[:, 0, :] = re.astype(BF16)
+    out_ref[:, 1, :] = im.astype(BF16)
 
 
 def first_back_kernel(prop_ref, piece_ref, out_ref):
     groups, double, lanes = out_ref.shape
     rows = double // 2
-    re, im = complex_dot(prop_ref[0], prop_ref[1], piece_ref[:, :lanes], piece_ref[:, lanes:])
+    re, im = complex_dot(prop_ref[0], prop_ref[1], piece_ref[:, 0, :], piece_ref[:, 1, :])
     out_ref[:, :rows, :] = re.astype(BF16).reshape(groups, rows, lanes)
     out_ref[:, rows:, :] = im.astype(BF16).reshape(groups, rows, lanes)
 
@@ -163,7 +165,7 @@
         for s in range(0, peers, 16):
             tiles = []
             for g in range(groups):
-                piece = piece_ref[g * peers + s:g * peers + s + 16, part * lanes:(part + 1) * lanes]
+                piece = piece_ref[g * peers + s:g * peers + s + 16, part, :]
                 piece = piece.astype(F32)
                 tiles.append([piece[:, h * LANES:(h + 1) * LANES] for h in range(lanes // LANES)])
             tiles = swap_blocks(tiles, width)
@@ -197,7 +199,7 @@
                 tiles.append([piece[:, h * LANES:(h + 1) * LANES] for h in range(channels // LANES)])
             tiles = swap_blocks(tiles, width)
             for g in range(groups):
-                out_ref[g * peers + s:g * peers + s + 16, part * lanes:(part + 1) * lanes] = (
+                out_ref[g * peers + s:g * peers + s + 16, part, :] = (
                     jnp.concatenate(tiles[g], axis=1).astype(BF16)
                 )
 
@@ -223,6 +225,21 @@
         out_ref[:, h * LANES:(h + 1) * LANES] = held[h].astype(BF16)
 
 
+def swap_rows(table, axis, step, last):
+    size = table.shape[0]
+    me = lax.axis_index(axis)
+    while step >= last:
+        pairs = [(i, i ^ step) for i in range(size)]
+        split = table.reshape(size // (2 * step), 2, step, table.shape[1])
+        low, high = split[:, 0], split[:, 1]
+        upper = (me & step) != 0
+        other = lax.ppermute(jnp.where(upper, low, high), axis, pairs)
+        low, high = jnp.where(upper, other, low), jnp.where(upper, high, other)
+        table = jnp.stack([low, high], axis=1).reshape(table.shape)
+        step //= 2
+    return table
+
+
 def on_device(amplitude, coupling, pattern, radial, first_prop, second_prop):
     _, rows, cols, channels = amplitude.shape
     cells = rows * cols
@@ -231,7 +248,7 @@
     width = channels // groups
     lanes = cols * width
     r1, r2 = first_prop.shape[1], second_prop.shape[1]
-    params = pltpu.CompilerParams(vmem_limit_bytes=48 * 1024 * 1024)
+    params = pltpu.CompilerParams(vmem_limit_bytes=20 * 1024 * 1024)
     vmem = pl.BlockSpec(memory_space=pltpu.VMEM)
     smem = pl.BlockSpec(memory_space=pltpu.SMEM)
     call = functools.partial(pl.pallas_call, compiler_params=params, out_specs=vmem)
@@ -239,35 +256,38 @@
 
     packed = radial.transpose(1, 0, 2).reshape(rows, terms * cols)
     packed = jnp.pad(packed, ((0, 0), (0, (-terms * cols) % LANES)))
-    packed = lax.all_to_all(packed, "rb", split_axis=0, concat_axis=0, tiled=True)
-
-    piece, weights, ordered = pl.pallas_call(
+
+    weights, ordered = pl.pallas_call(
+        functools.partial(tables_kernel, cols),
+        out_shape=[shape(coupling.shape, BF16), shape(second_prop.shape, BF16)],
+        in_specs=[vmem, smem, vmem],
+        out_specs=[vmem] * 2,
+        compiler_params=params,
+    )(coupling, pattern, second_prop)
+    packed = swap_rows(packed, "rb", peers // 2, peers // 2)
+    packed, weights = lax.optimization_barrier((packed, weights))
+    packed = swap_rows(packed, "rb", peers // 4, 1)
+    piece = call(
         functools.partial(first_kick_kernel, groups),
-        out_shape=[
-            shape((groups, 2 * rows, lanes), BF16),
-            shape(coupling.shape, BF16),
-            shape(second_prop.shape, BF16),
-        ],
-        in_specs=[vmem, vmem, smem, vmem, vmem],
-        out_specs=[vmem] * 3,
+        out_shape=shape((groups, 2 * rows, lanes), BF16),
+        in_specs=[vmem] * 3,
         scratch_shapes=[
             pltpu.VMEM((channels // LANES, 2 * cells, LANES), F32),
             pltpu.VMEM((2, cells, channels), BF16),
             pltpu.VMEM((2, cells, channels), F32),
         ],
-        compiler_params=params,
-    )(amplitude.reshape(2 * cells, channels), coupling, pattern, radial, second_prop)
-    piece, packed = lax.optimization_barrier((piece, packed))
+    )(amplitude.reshape(2 * cells, channels), weights, radial)
     piece = lax.all_to_all(piece, "ra", split_axis=0, concat_axis=0, tiled=True)
     half = call(
         first_forward_kernel,
-        out_shape=shape((r1, 2 * lanes), BF16),
+        out_shape=shape((r1, 2, lanes), BF16),
         in_specs=[vmem, vmem],
     )(first_prop, piece)
+    half, packed = lax.optimization_barrier((half, packed))
     half = lax.all_to_all(half, ("ra", "rb"), split_axis=0, concat_axis=0, tiled=True)
     half = call(
         functools.partial(second_kernel, groups, cols),
-        out_shape=shape((groups * peers, 2 * lanes), BF16),
+        out_shape=shape((groups * peers, 2, lanes), BF16),
         in_specs=[vmem] * 4,
         scratch_shapes=[pltpu.VMEM((2, r2, channels), BF16)] * 2,
     )(half, ordered, weights, packed)

time: 210 us -> 195 us (0.929)
  blocking collectives: 155 us -> 127 us
  starting transfers between devices: 21.1 us -> 37.9 us
  local copies, waits for them, and re-layouts: 11.8 us -> 3.47 us
  Pallas kernels: 12.3 us -> 16.3 us
  waiting for transfers between devices: 6.79 us -> 10.1 us
  other arithmetic: 2.53 us -> 0.08 us
    all_to_all x2 -> x1, blocking collectives: 63 us -> 30 us  [on_device(): piece = lax.all_to_all(piece, 'ra', split_axis=0, concat_axis=0, tiled=True)]
    ppermute x0 -> x5, starting transfers between devices: none -> 24 us  [swap_rows(): other = lax.ppermute(jnp.where(upper, low, high), axis, pairs)]
    ppermute x0 -> x5, waiting for transfers between devices: none -> 7.7 us  [swap_rows(): other = lax.ppermute(jnp.where(upper, low, high), axis, pairs)]
    all_to_all x1, starting transfers between devices: 21.1 us -> 13.9 us  [on_device(): piece = lax.all_to_all(piece, 'ra', split_axis=0, concat_axis=0, tiled=True)]
    unnamed x20 -> x15, local copies, waits for them, and re-layouts: 9.87 us -> 3.42 us
    all_to_all x2, blocking collectives: 91.9 us -> 96.8 us  [on_device(): lax.all_to_all(half, ('ra', 'rb'), split_axis=0, concat_axis=0, tiled=True)]
    all_to_all x1, waiting for transfers between devices: 6.79 us -> 2.38 us  [on_device(): piece = lax.all_to_all(piece, 'ra', split_axis=0, concat_axis=0, tiled=True)]
    pallas_call x2 -> x3, Pallas kernels: 5.4 us -> 8.04 us  [the longest x1 4.49 us: on_device(): call(functools.partial(first_kick_kernel, groups), out_shape=shape((group...]
  transfers between devices with their start and end apart: 1 -> 6, of which waited for: 1 -> 4; matrix products, arithmetic and copies ran while one was open for 0% -> 0% of each run, Pallas kernels for 2% -> 4%
where the time goes in v4:
time: 195 us
  blocking collectives  127 us (65%)
  starting transfers between devices  37.9 us (19%)
  Pallas kernels  16.3 us (8%)
  waiting for transfers between devices  10.1 us (5%)
  local copies, waits for them, and re-layouts  3.47 us (2%)
    all_to_all x2, blocking collectives, on_device(): lax.all_to_all(half, ('ra', 'rb'), split_axis=0, concat_axis=0, tiled=True)  96.8 us
    all_to_all x1, blocking collectives, on_device(): piece = lax.all_to_all(piece, 'ra', split_axis=0, concat_axis=0, tiled=True)  30 us
    ppermute x5, starting transfers between devices, swap_rows(): other = lax.ppermute(jnp.where(upper, low, high), axis, pairs)  24 us
    all_to_all x1, starting transfers between devices, on_device(): piece = lax.all_to_all(piece, 'ra', split_axis=0, concat_axis=0, tiled=True)  13.9 us
    ppermute x5, waiting for transfers between devices, swap_rows(): other = lax.ppermute(jnp.where(upper, low, high), axis, pairs)  7.7 us
    pallas_call x1, Pallas kernels, on_device(): call(functools.partial(second_kernel, groups, cols), out_shape=shape((gro...  5.01 us
    pallas_call x1, Pallas kernels, on_device(): call(functools.partial(first_kick_kernel, groups), out_shape=shape((group...  4.49 us
  transfers between devices with their start and end apart: 6, of which 4 were waited for; matrix products, arithmetic and copies ran while one was open for 0% of the time, Pallas kernels for 4%

profile of v4, /device:TPU:1, one launch (start us, length us, event | category | flops | bytes accessed | tf_op | source)
XLA Modules:
  0.0 194.9 jit_solution(10811714213109572021)
XLA Ops:
  0.0 0.9 copy.49
  0.9 0.0 copy-start.5
  0.9 5.5 %collective-permute-start = (f32[1,16,128]{2,1,0:T(8,128)S(1)}, f32[1,16,128]{2,1,0:T(8,128)S(1)}, u32[]{:S(2)}, u32[]{:S(2)}) collective-permute-start(f32[1,16,128]{2,1,0:T(8,128)S(1)} %fusion), channel_id=1, source_target_pairs={{0,16},{1,17},{2,18},{3,19},{4,20},{5,21},{6,22},{7,23},{8,24},{9,... | collective-permute-start | bytes 24584 | tf_op jit(solution)/shard_map/ppermute | solution.py:236
  6.4 0.0 copy-done.5
  6.4 0.1 copy.38.pattern_ref
  6.5 0.0 copy-start.1
  6.5 1.2 copy-done.1
  7.7 0.0 copy-start.2
  7.7 1.1 copy-done.2
  8.9 0.0 copy-start.3
  8.9 2.3 %shard_map.64 = (bf16[6,256,256]{2,1,0:T(8,128)(2,1)S(1)}, bf16[2,512,512]{2,1,0:T(8,128)(2,1)S(1)}) custom-call(bf16[6,256,256]{2,1,0:T(8,128)(2,1)S(1)} %copy-done.2, s32[6,4,4]{2,1,0:T(4,128)S(1)} %copy.38.pattern_ref, bf16[2,512,512]{2,1,0:T(8,128)(2,1)S(1)} %copy-done.1), custom_call_target="tpu_custom_call" | custom-call | tf_op jit(solution)/shard_map/pallas_call | solution.py:260
  11.2 0.0 copy-start.4
  11.2 0.0 collective-permute-done
  11.3 2.2 %collective-permute-start.1 = (f32[2,8,128]{2,1,0:T(8,128)S(1)}, f32[2,8,128]{2,1,0:T(8,128)S(1)}, u32[]{:S(2)}, u32[]{:S(2)}) collective-permute-start(f32[2,8,128]{2,1,0:T(8,128)S(1)} %fusion.1), channel_id=1, source_target_pairs={{0,8},{1,9},{2,10},{3,11},{4,12},{5,13},{6,14},{7,15},{8,0},{9,1},... | collective-permute-start | bytes 24584 | tf_op jit(solution)/shard_map/ppermute | solution.py:236
  13.5 0.0 copy-done.4
  13.5 0.1 copy.39.radial_ref
  13.6 0.0 copy-done.3
  13.6 4.5 %shard_map.65 = bf16[16,64,256]{2,1,0:T(8,128)(2,1)} custom-call(bf16[1024,256]{1,0:T(8,128)(2,1)S(1)} %bitcast.98, bf16[6,256,256]{2,1,0:T(8,128)(2,1)S(1)} %get-tuple-element.12.weights_ref, f32[6,32,16]{2,1,0:T(8,128)S(1)} %copy.39.radial_ref), custom_call_target="tpu_custom_call" | custom-call | tf_op jit(solution)/shard_map/pallas_call | solution.py:270
  18.1 0.0 copy-start
  18.1 13.9 %all-to-all-start = ((bf16[16,64,256]{2,1,0:T(8,128)(2,1)}), bf16[16,64,256]{2,1,0:T(8,128)(2,1)S(1)}, u32[]{:S(2)}, u32[]{:S(2)}) async-start(bf16[16,64,256]{2,1,0:T(8,128)(2,1)} %shard_map.65), calls=%async_computation | async-start | bytes 1048576 | tf_op jit(solution)/shard_map/all_to_all | solution.py:280
  32.0 0.0 collective-permute-done.1
  32.1 4.8 %collective-permute-start.2 = (f32[4,4,128]{2,1,0:T(4,128)S(1)}, f32[4,4,128]{2,1,0:T(4,128)S(1)}, u32[]{:S(2)}, u32[]{:S(2)}) collective-permute-start(f32[4,4,128]{2,1,0:T(4,128)S(1)} %fusion.4), channel_id=1, source_target_pairs={{0,4},{1,5},{2,6},{3,7},{4,0},{5,1},{6,2},{7,3},{8,12},{9,13},{10,... | collective-permute-start | bytes 24584 | tf_op jit(solution)/shard_map/ppermute | solution.py:236
  36.9 1.1 collective-permute-done.2
  38.1 3.5 %collective-permute-start.3 = (f32[8,2,128]{2,0,1:T(8,128)S(1)}, f32[8,2,128]{2,0,1:T(8,128)S(1)}, u32[]{:S(2)}, u32[]{:S(2)}) collective-permute-start(f32[8,2,128]{2,0,1:T(8,128)S(1)} %fusion.2), channel_id=1, source_target_pairs={{0,2},{1,3},{2,0},{3,1},{4,6},{5,7},{6,4},{7,5},{8,10},{9,11},{10,... | collective-permute-start | bytes 24584 | tf_op jit(solution)/shard_map/ppermute | solution.py:236
  41.6 1.3 collective-permute-done.3
  42.9 7.9 %collective-permute-start.4 = (f32[16,1,128]{2,0,1:T(8,128)S(1)}, f32[16,1,128]{2,0,1:T(8,128)S(1)}, u32[]{:S(2)}, u32[]{:S(2)}) collective-permute-start(f32[16,1,128]{2,0,1:T(8,128)S(1)} %fusion.3), channel_id=1, source_target_pairs={{0,1},{1,0},{2,3},{3,2},{4,5},{5,4},{6,7},{7,6},{8,9},{9,8},{10,11... | collective-permute-start | bytes 24584 | tf_op jit(solution)/shard_map/ppermute | solution.py:236
  50.9 5.3 %collective-permute-done.4 = f32[16,1,128]{2,0,1:T(8,128)S(1)} collective-permute-done((f32[16,1,128]{2,0,1:T(8,128)S(1)}, f32[16,1,128]{2,0,1:T(8,128)S(1)}, u32[]{:S(2)}, u32[]{:S(2)}) %collective-permute-start.4) | collective-permute-done | bytes 8224 | tf_op jit(solution)/shard_map/ppermute | solution.py:236
  56.2 2.4 %all-to-all-done.piece_ref = bf16[16,64,256]{2,1,0:T(8,128)(2,1)S(1)} async-done(((bf16[16,64,256]{2,1,0:T(8,128)(2,1)}), bf16[16,64,256]{2,1,0:T(8,128)(2,1)S(1)}, u32[]{:S(2)}, u32[]{:S(2)}) %all-to-all-start) | async-done | bytes 524320 | tf_op jit(solution)/shard_map/all_to_all | solution.py:280
  58.6 0.0 copy-done
  58.6 1.2 shard_map.66
  59.8 52.8 %all_to_all.20.piece_ref = bf16[512,2,256]{2,1,0:T(2,128)(2,1)S(1)} all-to-all(bf16[512,2,256]{2,1,0:T(2,128)(2,1)S(1)} %shard_map.66), channel_id=1, replica_groups=mesh['ra'=16,'rb'=32] {'ra','rb'}, dimensions={0} | all-to-all | bytes 1048576 | tf_op jit(solution)/shard_map/all_to_all | solution.py:287
  112.6 5.0 %shard_map.67 = bf16[512,2,256]{2,1,0:T(2,128)(2,1)S(1)} custom-call(bf16[512,2,256]{2,1,0:T(2,128)(2,1)S(1)} %all_to_all.20.piece_ref, bf16[2,512,512]{2,1,0:T(8,128)(2,1)S(1)} %get-tuple-element.15.prop_ref, bf16[6,256,256]{2,1,0:T(8,128)(2,1)S(1)} %get-tuple-element.12.weights_ref, f32[32,128]{1,0:T(8,128)S(1)} %bitcast.99), custom_call_target="tpu_custom_call" | custom-call | tf_op jit(solution)/shard_map/pallas_call | solution.py:288
  117.6 44.0 %all_to_all.21.piece_ref = bf16[512,2,256]{2,1,0:T(2,128)(2,1)S(1)} all-to-all(bf16[512,2,256]{2,1,0:T(2,128)(2,1)S(1)} %shard_map.67), channel_id=1, replica_groups=mesh['ra'=16,'rb'=32] {'ra','rb'}, dimensions={0} | all-to-all | bytes 1048576 | tf_op jit(solution)/shard_map/all_to_all | solution.py:294
  161.6 1.5 shard_map.68
  163.1 30.0 %all_to_all.22.piece_ref = bf16[16,64,256]{2,1,0:T(8,128)(2,1)S(1)} all-to-all(bf16[16,64,256]{2,1,0:T(8,128)(2,1)S(1)} %shard_map.68), channel_id=1, replica_groups=mesh['ra'=16,'rb'=32] {'ra'}, dimensions={0} | all-to-all | bytes 1048576 | tf_op jit(solution)/shard_map/all_to_all | solution.py:300
  193.0 1.8 shard_map.69
  (20 shorter events, 0.1 us)
Async XLA Ops:
  0.9 5.5 %copy-start.5 = (s32[6,4,4]{0,2,1:T(4,128)S(1)}, s32[6,4,4]{0,2,1:T(4,128)}, u32[]{:S(2)}) copy-start(s32[6,4,4]{0,2,1:T(4,128)} %param.8) | copy-start | bytes 1156
  0.9 10.3 %collective-permute-start = (f32[1,16,128]{2,1,0:T(8,128)S(1)}, f32[1,16,128]{2,1,0:T(8,128)S(1)}, u32[]{:S(2)}, u32[]{:S(2)}) collective-permute-start(f32[1,16,128]{2,1,0:T(8,128)S(1)} %fusion), channel_id=1, source_target_pairs={{0,16},{1,17},{2,18},{3,19},{4,20},{5,21},{6,22},{7,23},{8,24},{9,... | collective-permute-start | bytes 24584 | tf_op jit(solution)/shard_map/ppermute | solution.py:236
  6.5 1.2 copy-start.1
  7.7 1.1 copy-start.2
  8.9 4.8 %copy-start.3 = (bf16[2,32,16,256]{3,2,1,0:T(8,128)(2,1)S(1)}, bf16[2,32,16,256]{3,2,1,0:T(8,128)(2,1)}, u32[]{:S(2)}) copy-start(bf16[2,32,16,256]{3,2,1,0:T(8,128)(2,1)} %param.6) | copy-start | bytes 1572868
  11.2 2.3 %copy-start.4 = (f32[6,32,16]{1,2,0:T(8,128)S(1)}, f32[6,32,16]{1,2,0:T(8,128)}, u32[]{:S(2)}) copy-start(f32[6,32,16]{1,2,0:T(8,128)} %param.9) | copy-start | bytes 36868
  11.3 20.7 %collective-permute-start.1 = (f32[2,8,128]{2,1,0:T(8,128)S(1)}, f32[2,8,128]{2,1,0:T(8,128)S(1)}, u32[]{:S(2)}, u32[]{:S(2)}) collective-permute-start(f32[2,8,128]{2,1,0:T(8,128)S(1)} %fusion.1), channel_id=1, source_target_pairs={{0,8},{1,9},{2,10},{3,11},{4,12},{5,13},{6,14},{7,15},{8,0},{9,1},... | collective-permute-start | bytes 24584 | tf_op jit(solution)/shard_map/ppermute | solution.py:236
  18.1 40.5 %copy-start = (bf16[2,512,512]{2,1,0:T(8,128)(2,1)S(1)}, bf16[2,512,512]{2,1,0:T(8,128)(2,1)}, u32[]{:S(2)}) copy-start(bf16[2,512,512]{2,1,0:T(8,128)(2,1)} %prop_ref.5) | copy-start | bytes 3145732
  18.1 40.5 %all-to-all-start = ((bf16[16,64,256]{2,1,0:T(8,128)(2,1)}), bf16[16,64,256]{2,1,0:T(8,128)(2,1)S(1)}, u32[]{:S(2)}, u32[]{:S(2)}) async-start(bf16[16,64,256]{2,1,0:T(8,128)(2,1)} %shard_map.65), calls=%async_computation | async-start | bytes 1048576 | tf_op jit(solution)/shard_map/all_to_all | solution.py:280
  32.1 5.9 %collective-permute-start.2 = (f32[4,4,128]{2,1,0:T(4,128)S(1)}, f32[4,4,128]{2,1,0:T(4,128)S(1)}, u32[]{:S(2)}, u32[]{:S(2)}) collective-permute-start(f32[4,4,128]{2,1,0:T(4,128)S(1)} %fusion.4), channel_id=1, source_target_pairs={{0,4},{1,5},{2,6},{3,7},{4,0},{5,1},{6,2},{7,3},{8,12},{9,13},{10,... | collective-permute-start | bytes 24584 | tf_op jit(solution)/shard_map/ppermute | solution.py:236
  38.1 4.8 %collective-permute-start.3 = (f32[8,2,128]{2,0,1:T(8,128)S(1)}, f32[8,2,128]{2,0,1:T(8,128)S(1)}, u32[]{:S(2)}, u32[]{:S(2)}) collective-permute-start(f32[8,2,128]{2,0,1:T(8,128)S(1)} %fusion.2), channel_id=1, source_target_pairs={{0,2},{1,3},{2,0},{3,1},{4,6},{5,7},{6,4},{7,5},{8,10},{9,11},{10,... | collective-permute-start | bytes 24584 | tf_op jit(solution)/shard_map/ppermute | solution.py:236
  42.9 13.2 %collective-permute-start.4 = (f32[16,1,128]{2,0,1:T(8,128)S(1)}, f32[16,1,128]{2,0,1:T(8,128)S(1)}, u32[]{:S(2)}, u32[]{:S(2)}) collective-permute-start(f32[16,1,128]{2,0,1:T(8,128)S(1)} %fusion.3), channel_id=1, source_target_pairs={{0,1},{1,0},{2,3},{3,2},{4,5},{5,4},{6,7},{7,6},{8,9},{9,8},{10,11... | collective-permute-start | bytes 24584 | tf_op jit(solution)/shard_map/ppermute | solution.py:236

commit v5 on v4

--- a/solution.py
+++ b/solution.py
@@ -90,19 +90,20 @@
     return [value[:, h * LANES:(h + 1) * LANES] for h in range(value.shape[1] // LANES)]
 
 
-def tables_kernel(inner, coupling_ref, pattern_ref, prop_ref, weights_ref, ordered_ref):
-    block = coupling_ref.shape[1] // pattern_ref.shape[1]
-    for k in range(coupling_ref.shape[0]):
-        weights_ref[k] = masked_weights(coupling_ref, pattern_ref, k, block)
+def order_kernel(inner, prop_ref, ordered_ref):
     order(prop_ref, ordered_ref, inner)
 
 
-def first_kick_kernel(groups, amp_ref, weights_ref, radial_ref, out_ref, held, moved, kicked):
+def first_kick_kernel(groups, amp_ref, coupling_ref, pattern_ref, radial_ref, out_ref, weights_ref,
+                      held, moved, kicked):
     terms, rows, cols = radial_ref.shape
     cells = rows * cols
-    channels = weights_ref.shape[1]
+    channels = coupling_ref.shape[1]
+    block = channels // pattern_ref.shape[1]
     parts = channels // LANES
-    weights = [weights_ref[k] for k in range(terms)]
+    weights = [masked_weights(coupling_ref, pattern_ref, k, block) for k in range(terms)]
+    for k in range(terms):
+        weights_ref[k] = weights[k]
     for h in range(parts):
         held[h] = amp_ref[:, h * LANES:(h + 1) * LANES].astype(F32)
     for part in range(2):
@@ -225,10 +226,10 @@
         out_ref[:, h * LANES:(h + 1) * LANES] = held[h].astype(BF16)
 
 
-def swap_rows(table, axis, step, last):
+def swap_rows(table, axis, steps):
     size = table.shape[0]
     me = lax.axis_index(axis)
-    while step >= last:
+    for step in steps:
         pairs = [(i, i ^ step) for i in range(size)]
         split = table.reshape(size // (2 * step), 2, step, table.shape[1])
         low, high = split[:, 0], split[:, 1]
@@ -236,7 +237,6 @@
         other = lax.ppermute(jnp.where(upper, low, high), axis, pairs)
         low, high = jnp.where(upper, other, low), jnp.where(upper, high, other)
         table = jnp.stack([low, high], axis=1).reshape(table.shape)
-        step //= 2
     return table
 
 
@@ -257,33 +257,34 @@
     packed = radial.transpose(1, 0, 2).reshape(rows, terms * cols)
     packed = jnp.pad(packed, ((0, 0), (0, (-terms * cols) % LANES)))
 
-    weights, ordered = pl.pallas_call(
-        functools.partial(tables_kernel, cols),
-        out_shape=[shape(coupling.shape, BF16), shape(second_prop.shape, BF16)],
-        in_specs=[vmem, smem, vmem],
+    packed = swap_rows(packed, "rb", [1])
+    piece, weights = pl.pallas_call(
+        functools.partial(first_kick_kernel, groups),
+        out_shape=[shape((groups, 2 * rows, lanes), BF16), shape(coupling.shape, BF16)],
+        in_specs=[vmem, vmem, smem, vmem],
         out_specs=[vmem] * 2,
-        compiler_params=params,
-    )(coupling, pattern, second_prop)
-    packed = swap_rows(packed, "rb", peers // 2, peers // 2)
-    packed, weights = lax.optimization_barrier((packed, weights))
-    packed = swap_rows(packed, "rb", peers // 4, 1)
-    piece = call(
-        functools.partial(first_kick_kernel, groups),
-        out_shape=shape((groups, 2 * rows, lanes), BF16),
-        in_specs=[vmem] * 3,
         scratch_shapes=[
             pltpu.VMEM((channels // LANES, 2 * cells, LANES), F32),
             pltpu.VMEM((2, cells, channels), BF16),
             pltpu.VMEM((2, cells, channels), F32),
         ],
-    )(amplitude.reshape(2 * cells, channels), weights, radial)
+        compiler_params=params,
+    )(amplitude.reshape(2 * cells, channels), coupling, pattern, radial)
+    packed, weights, second_prop = lax.optimization_barrier((packed, weights, second_prop))
+    steps = [1 << bit for bit in range(1, peers.bit_length() - 1)]
+    packed = swap_rows(packed, "rb", steps[::-1])
+    ordered = call(
+        functools.partial(order_kernel, cols),
+        out_shape=shape(second_prop.shape, BF16),
+        in_specs=[vmem],
+    )(second_prop)
     piece = lax.all_to_all(piece, "ra", split_axis=0, concat_axis=0, tiled=True)
     half = call(
         first_forward_kernel,
         out_shape=shape((r1, 2, lanes), BF16),
         in_specs=[vmem, vmem],
     )(first_prop, piece)
-    half, packed = lax.optimization_barrier((half, packed))
+    half, packed, ordered = lax.optimization_barrier((half, packed, ordered))
     half = lax.all_to_all(half, ("ra", "rb"), split_axis=0, concat_axis=0, tiled=True)
     half = call(
         functools.partial(second_kernel, groups, cols),

time: 195 us -> 194 us (level)
  waiting for transfers between devices: 10.1 us -> 6.65 us
    ppermute x5, starting transfers between devices: 24 us -> 32.8 us  [swap_rows(): other = lax.ppermute(jnp.where(upper, low, high), axis, pairs)]
    all_to_all x1, starting transfers between devices: 13.9 us -> 5.99 us  [on_device(): piece = lax.all_to_all(piece, 'ra', split_axis=0, concat_axis=0, tiled=True)]
    ppermute x5, waiting for transfers between devices: 7.7 us -> 3.61 us  [swap_rows(): other = lax.ppermute(jnp.where(upper, low, high), axis, pairs)]
  transfers between devices with their start and end apart: 6 -> 6, of which waited for: 4 -> 4; matrix products, arithmetic and copies ran while one was open for 0% -> 0% of each run, Pallas kernels for 4% -> 3%
where the time goes in v5:
time: 194 us; the launch traced here: 193 us
  blocking collectives  127 us (65%)
  starting transfers between devices  38.8 us (20%)
  Pallas kernels  16.2 us (8%)
  waiting for transfers between devices  6.65 us (3%)
  local copies, waits for them, and re-layouts  4.52 us (2%)
    all_to_all x2, blocking collectives, on_device(): lax.all_to_all(half, ('ra', 'rb'), split_axis=0, concat_axis=0, tiled=True)  96.6 us
    ppermute x5, starting transfers between devices, swap_rows(): other = lax.ppermute(jnp.where(upper, low, high), axis, pairs)  32.8 us
    all_to_all x1, blocking collectives, on_device(): piece = lax.all_to_all(piece, 'ra', split_axis=0, concat_axis=0, tiled=True)  30 us
    all_to_all x1, starting transfers between devices, on_device(): piece = lax.all_to_all(piece, 'ra', split_axis=0, concat_axis=0, tiled=True)  5.99 us
    pallas_call x1, Pallas kernels, on_device(): pl.pallas_call(functools.partial(first_kick_kernel, groups), out_shape=[s...  5.27 us
    pallas_call x1, Pallas kernels, on_device(): call(functools.partial(second_kernel, groups, cols), out_shape=shape((gro...  5.01 us
    unnamed x15, local copies, waits for them, and re-layouts  4.46 us
  transfers between devices with their start and end apart: 6, of which 4 were waited for; matrix products, arithmetic and copies ran while one was open for 0% of the time, Pallas kernels for 3%

profile of v5, /device:TPU:1, one launch (start us, length us, event | category | flops | bytes accessed | tf_op | source)
XLA Modules:
  0.0 193.1 jit_solution(2677099980561992710)
XLA Ops:
  0.0 0.9 copy.28
  0.9 0.0 copy-start.4
  0.9 0.0 copy-start.5
  0.9 16.3 %collective-permute-start = (f32[16,1,128]{2,0,1:T(8,128)S(1)}, f32[16,1,128]{2,0,1:T(8,128)S(1)}, u32[]{:S(2)}, u32[]{:S(2)}) collective-permute-start(f32[16,1,128]{2,0,1:T(8,128)S(1)} %broadcast_select_fusion), channel_id=1, source_target_pairs={{0,1},{1,0},{2,3},{3,2},{4,5},{5,4},{6,7},{7,6},{8,9},{9,8},{10,11... | collective-permute-start | bytes 24584 | tf_op jit(solution)/shard_map/ppermute | solution.py:237
  17.2 0.0 copy-done.4
  17.2 0.1 copy.20.radial_ref
  17.3 0.0 copy-done.5
  17.3 0.1 copy.19.pattern_ref
  17.4 0.0 copy-start.2
  17.4 1.1 copy-done.2
  18.6 0.0 copy-start.3
  18.6 1.0 copy-done.3
  19.6 5.3 %shard_map.64 = (bf16[16,64,256]{2,1,0:T(8,128)(2,1)}, bf16[6,256,256]{2,1,0:T(8,128)(2,1)S(1)}) custom-call(bf16[1024,256]{1,0:T(8,128)(2,1)S(1)} %bitcast.85, bf16[6,256,256]{2,1,0:T(8,128)(2,1)S(1)} %copy-done.2, s32[6,4,4]{2,1,0:T(4,128)S(1)} %copy.19.pattern_ref, f32[6,32,16]{2,1,0:T(8,128)S(1)} %copy.20.radial_ref), custom_call_target="tpu_custom_call" | custom-call | tf_op jit(solution)/shard_map/pallas_call | solution.py:261
  24.9 6.0 %all-to-all-start = ((bf16[16,64,256]{2,1,0:T(8,128)(2,1)}), bf16[16,64,256]{2,1,0:T(8,128)(2,1)S(1)}, u32[]{:S(2)}, u32[]{:S(2)}) async-start(bf16[16,64,256]{2,1,0:T(8,128)(2,1)} %get-tuple-element.13), calls=%async_computation | async-start | bytes 1048576 | tf_op jit(solution)/shard_map/all_to_all | solution.py:281
  30.9 0.0 collective-permute-done
  30.9 4.7 %collective-permute-start.1 = (f32[1,16,128]{2,1,0:T(8,128)S(1)}, f32[1,16,128]{2,1,0:T(8,128)S(1)}, u32[]{:S(2)}, u32[]{:S(2)}) collective-permute-start(f32[1,16,128]{2,1,0:T(8,128)S(1)} %fusion.3), channel_id=1, source_target_pairs={{0,16},{1,17},{2,18},{3,19},{4,20},{5,21},{6,22},{7,23},{8,24},{9,... | collective-permute-start | bytes 24584 | tf_op jit(solution)/shard_map/ppermute | solution.py:237
  35.6 1.2 collective-permute-done.1
  36.9 3.4 %collective-permute-start.2 = (f32[2,8,128]{2,1,0:T(8,128)S(1)}, f32[2,8,128]{2,1,0:T(8,128)S(1)}, u32[]{:S(2)}, u32[]{:S(2)}) collective-permute-start(f32[2,8,128]{2,1,0:T(8,128)S(1)} %broadcast_select_fusion.1), channel_id=1, source_target_pairs={{0,8},{1,9},{2,10},{3,11},{4,12},{5,13},{6,14},{7,15},{8,0},{9,1},... | collective-permute-start | bytes 24584 | tf_op jit(solution)/shard_map/ppermute | solution.py:237
  40.3 1.3 collective-permute-done.2
  41.6 4.8 %collective-permute-start.3 = (f32[4,4,128]{2,1,0:T(4,128)S(1)}, f32[4,4,128]{2,1,0:T(4,128)S(1)}, u32[]{:S(2)}, u32[]{:S(2)}) collective-permute-start(f32[4,4,128]{2,1,0:T(4,128)S(1)} %fusion.5), channel_id=1, source_target_pairs={{0,4},{1,5},{2,6},{3,7},{4,0},{5,1},{6,2},{7,3},{8,12},{9,13},{10,... | collective-permute-start | bytes 24584 | tf_op jit(solution)/shard_map/ppermute | solution.py:237
  46.5 1.1 collective-permute-done.3
  47.6 0.0 copy-start
  47.6 3.6 %collective-permute-start.4 = (f32[8,2,128]{2,0,1:T(8,128)S(1)}, f32[8,2,128]{2,0,1:T(8,128)S(1)}, u32[]{:S(2)}, u32[]{:S(2)}) collective-permute-start(f32[8,2,128]{2,0,1:T(8,128)S(1)} %fusion.4), channel_id=1, source_target_pairs={{0,2},{1,3},{2,0},{3,1},{4,6},{5,7},{6,4},{7,5},{8,10},{9,11},{10,... | collective-permute-start | bytes 24584 | tf_op jit(solution)/shard_map/ppermute | solution.py:237
  51.2 0.0 copy-start.1
  51.2 1.2 copy-done.1
  52.5 1.5 shard_map.66.prop_ref
  53.9 0.0 collective-permute-done.4
  54.0 3.0 %all-to-all-done.piece_ref = bf16[16,64,256]{2,1,0:T(8,128)(2,1)S(1)} async-done(((bf16[16,64,256]{2,1,0:T(8,128)(2,1)}), bf16[16,64,256]{2,1,0:T(8,128)(2,1)S(1)}, u32[]{:S(2)}, u32[]{:S(2)}) %all-to-all-start) | async-done | bytes 524320 | tf_op jit(solution)/shard_map/all_to_all | solution.py:281
  57.0 0.0 copy-done
  57.0 1.2 shard_map.65
  58.2 52.6 %all_to_all.20.piece_ref = bf16[512,2,256]{2,1,0:T(2,128)(2,1)S(1)} all-to-all(bf16[512,2,256]{2,1,0:T(2,128)(2,1)S(1)} %shard_map.65), channel_id=1, replica_groups=mesh['ra'=16,'rb'=32] {'ra','rb'}, dimensions={0} | all-to-all | bytes 1048576 | tf_op jit(solution)/shard_map/all_to_all | solution.py:288
  110.8 5.0 %shard_map.67 = bf16[512,2,256]{2,1,0:T(2,128)(2,1)S(1)} custom-call(bf16[512,2,256]{2,1,0:T(2,128)(2,1)S(1)} %all_to_all.20.piece_ref, bf16[2,512,512]{2,1,0:T(8,128)(2,1)S(1)} %shard_map.66.prop_ref, bf16[6,256,256]{2,1,0:T(8,128)(2,1)S(1)} %get-tuple-element.19.weights_ref, f32[32,128]{1,0:T(8,128)S(1)} %bitcast.86), custom_call_target="tpu_custom_call" | custom-call | tf_op jit(solution)/shard_map/pallas_call | solution.py:289
  115.9 44.0 %all_to_all.21.piece_ref = bf16[512,2,256]{2,1,0:T(2,128)(2,1)S(1)} all-to-all(bf16[512,2,256]{2,1,0:T(2,128)(2,1)S(1)} %shard_map.67), channel_id=1, replica_groups=mesh['ra'=16,'rb'=32] {'ra','rb'}, dimensions={0} | all-to-all | bytes 1048576 | tf_op jit(solution)/shard_map/all_to_all | solution.py:295
  159.8 1.5 shard_map.68
  161.3 30.0 %all_to_all.22.piece_ref = bf16[16,64,256]{2,1,0:T(8,128)(2,1)S(1)} all-to-all(bf16[16,64,256]{2,1,0:T(8,128)(2,1)S(1)} %shard_map.68), channel_id=1, replica_groups=mesh['ra'=16,'rb'=32] {'ra'}, dimensions={0} | all-to-all | bytes 1048576 | tf_op jit(solution)/shard_map/all_to_all | solution.py:301
  191.3 1.8 shard_map.69
  (19 shorter events, 0.1 us)
Async XLA Ops:
  0.9 16.4 %copy-start.4 = (f32[6,32,16]{1,2,0:T(8,128)S(1)}, f32[6,32,16]{1,2,0:T(8,128)}, u32[]{:S(2)}) copy-start(f32[6,32,16]{1,2,0:T(8,128)} %param.9) | copy-start | bytes 36868
  0.9 16.4 %copy-start.5 = (s32[6,4,4]{0,2,1:T(4,128)S(1)}, s32[6,4,4]{0,2,1:T(4,128)}, u32[]{:S(2)}) copy-start(s32[6,4,4]{0,2,1:T(4,128)} %param.8) | copy-start | bytes 1156
  0.9 29.9 %collective-permute-start = (f32[16,1,128]{2,0,1:T(8,128)S(1)}, f32[16,1,128]{2,0,1:T(8,128)S(1)}, u32[]{:S(2)}, u32[]{:S(2)}) collective-permute-start(f32[16,1,128]{2,0,1:T(8,128)S(1)} %broadcast_select_fusion), channel_id=1, source_target_pairs={{0,1},{1,0},{2,3},{3,2},{4,5},{5,4},{6,7},{7,6},{8,9},{9,8},{10,11... | collective-permute-start | bytes 24584 | tf_op jit(solution)/shard_map/ppermute | solution.py:237
  17.4 1.1 copy-start.2
  18.6 1.0 copy-start.3
  24.9 32.2 %all-to-all-start = ((bf16[16,64,256]{2,1,0:T(8,128)(2,1)}), bf16[16,64,256]{2,1,0:T(8,128)(2,1)S(1)}, u32[]{:S(2)}, u32[]{:S(2)}) async-start(bf16[16,64,256]{2,1,0:T(8,128)(2,1)} %get-tuple-element.13), calls=%async_computation | async-start | bytes 1048576 | tf_op jit(solution)/shard_map/all_to_all | solution.py:281
  30.9 5.9 %collective-permute-start.1 = (f32[1,16,128]{2,1,0:T(8,128)S(1)}, f32[1,16,128]{2,1,0:T(8,128)S(1)}, u32[]{:S(2)}, u32[]{:S(2)}) collective-permute-start(f32[1,16,128]{2,1,0:T(8,128)S(1)} %fusion.3), channel_id=1, source_target_pairs={{0,16},{1,17},{2,18},{3,19},{4,20},{5,21},{6,22},{7,23},{8,24},{9,... | collective-permute-start | bytes 24584 | tf_op jit(solution)/shard_map/ppermute | solution.py:237
  36.9 4.7 %collective-permute-start.2 = (f32[2,8,128]{2,1,0:T(8,128)S(1)}, f32[2,8,128]{2,1,0:T(8,128)S(1)}, u32[]{:S(2)}, u32[]{:S(2)}) collective-permute-start(f32[2,8,128]{2,1,0:T(8,128)S(1)} %broadcast_select_fusion.1), channel_id=1, source_target_pairs={{0,8},{1,9},{2,10},{3,11},{4,12},{5,13},{6,14},{7,15},{8,0},{9,1},... | collective-permute-start | bytes 24584 | tf_op jit(solution)/shard_map/ppermute | solution.py:237
  41.6 5.9 %collective-permute-start.3 = (f32[4,4,128]{2,1,0:T(4,128)S(1)}, f32[4,4,128]{2,1,0:T(4,128)S(1)}, u32[]{:S(2)}, u32[]{:S(2)}) collective-permute-start(f32[4,4,128]{2,1,0:T(4,128)S(1)} %fusion.5), channel_id=1, source_target_pairs={{0,4},{1,5},{2,6},{3,7},{4,0},{5,1},{6,2},{7,3},{8,12},{9,13},{10,... | collective-permute-start | bytes 24584 | tf_op jit(solution)/shard_map/ppermute | solution.py:237
  47.6 9.5 %copy-start = (bf16[2,512,512]{2,1,0:T(8,128)(2,1)S(1)}, bf16[2,512,512]{2,1,0:T(8,128)(2,1)}, u32[]{:S(2)}) copy-start(bf16[2,512,512]{2,1,0:T(8,128)(2,1)} %prop_ref.4) | copy-start | bytes 3145732
  47.6 6.3 %collective-permute-start.4 = (f32[8,2,128]{2,0,1:T(8,128)S(1)}, f32[8,2,128]{2,0,1:T(8,128)S(1)}, u32[]{:S(2)}, u32[]{:S(2)}) collective-permute-start(f32[8,2,128]{2,0,1:T(8,128)S(1)} %fusion.4), channel_id=1, source_target_pairs={{0,2},{1,3},{2,0},{3,1},{4,6},{5,7},{6,4},{7,5},{8,10},{9,11},{10,... | collective-permute-start | bytes 24584 | tf_op jit(solution)/shard_map/ppermute | solution.py:237
  51.2 1.2 copy-start.1

commit v6 on v5

--- a/solution.py
+++ b/solution.py
@@ -62,7 +62,7 @@
 
 
 def kick_into(load, weights, factor_of, rows, count, store):
-    together = max(1, 128 // rows)
+    together = max(1, 512 // rows)
     for first in range(0, count, together):
         blocks = range(first, first + together)
         re, im = load(first * rows, together * rows)

time: 194 us -> 191 us (0.985)
  Pallas kernels: 16.2 us -> 13.3 us
where the time goes in v6:
time: 191 us; the launch traced here: 190 us
  blocking collectives  127 us (66%)
  starting transfers between devices  38.8 us (20%)
  Pallas kernels  13.3 us (7%)
  waiting for transfers between devices  6.66 us (3%)
  local copies, waits for them, and re-layouts  4.52 us (2%)
    all_to_all x2, blocking collectives, on_device(): lax.all_to_all(half, ('ra', 'rb'), split_axis=0, concat_axis=0, tiled=True)  96.7 us
    ppermute x5, starting transfers between devices, swap_rows(): other = lax.ppermute(jnp.where(upper, low, high), axis, pairs)  32.8 us
    all_to_all x1, blocking collectives, on_device(): piece = lax.all_to_all(piece, 'ra', split_axis=0, concat_axis=0, tiled=True)  29.9 us
    all_to_all x1, starting transfers between devices, on_device(): piece = lax.all_to_all(piece, 'ra', split_axis=0, concat_axis=0, tiled=True)  5.99 us
    unnamed x15, local copies, waits for them, and re-layouts  4.46 us
    pallas_call x1, Pallas kernels, on_device(): call(functools.partial(second_kernel, groups, cols), out_shape=shape((gro...  4.01 us
  transfers between devices with their start and end apart: 6, of which 4 were waited for; matrix products, arithmetic and copies ran while one was open for 0% of the time, Pallas kernels for 3%

profile of v6, /device:TPU:1, one launch (start us, length us, event | category | flops | bytes accessed | tf_op | source)
XLA Modules:
  0.0 190.3 jit_solution(13891151077693409051)
XLA Ops:
  0.0 0.9 copy.28
  0.9 0.0 copy-start.4
  0.9 0.0 copy-start.5
  0.9 16.3 %collective-permute-start = (f32[16,1,128]{2,0,1:T(8,128)S(1)}, f32[16,1,128]{2,0,1:T(8,128)S(1)}, u32[]{:S(2)}, u32[]{:S(2)}) collective-permute-start(f32[16,1,128]{2,0,1:T(8,128)S(1)} %broadcast_select_fusion), channel_id=1, source_target_pairs={{0,1},{1,0},{2,3},{3,2},{4,5},{5,4},{6,7},{7,6},{8,9},{9,8},{10,11... | collective-permute-start | bytes 24584 | tf_op jit(solution)/shard_map/ppermute | solution.py:237
  17.2 0.0 copy-done.4
  17.2 0.1 copy.20.radial_ref
  17.3 0.0 copy-done.5
  17.3 0.1 copy.19.pattern_ref
  17.4 0.0 copy-start.2
  17.4 1.1 copy-done.2
  18.6 0.0 copy-start.3
  18.6 1.0 copy-done.3
  19.6 3.4 %shard_map.64 = (bf16[16,64,256]{2,1,0:T(8,128)(2,1)}, bf16[6,256,256]{2,1,0:T(8,128)(2,1)S(1)}) custom-call(bf16[1024,256]{1,0:T(8,128)(2,1)S(1)} %bitcast.85, bf16[6,256,256]{2,1,0:T(8,128)(2,1)S(1)} %copy-done.2, s32[6,4,4]{2,1,0:T(4,128)S(1)} %copy.19.pattern_ref, f32[6,32,16]{2,1,0:T(8,128)S(1)} %copy.20.radial_ref), custom_call_target="tpu_custom_call" | custom-call | tf_op jit(solution)/shard_map/pallas_call | solution.py:261
  23.0 6.0 %all-to-all-start = ((bf16[16,64,256]{2,1,0:T(8,128)(2,1)}), bf16[16,64,256]{2,1,0:T(8,128)(2,1)S(1)}, u32[]{:S(2)}, u32[]{:S(2)}) async-start(bf16[16,64,256]{2,1,0:T(8,128)(2,1)} %get-tuple-element.13), calls=%async_computation | async-start | bytes 1048576 | tf_op jit(solution)/shard_map/all_to_all | solution.py:281
  29.0 0.0 collective-permute-done
  29.0 4.7 %collective-permute-start.1 = (f32[1,16,128]{2,1,0:T(8,128)S(1)}, f32[1,16,128]{2,1,0:T(8,128)S(1)}, u32[]{:S(2)}, u32[]{:S(2)}) collective-permute-start(f32[1,16,128]{2,1,0:T(8,128)S(1)} %fusion.3), channel_id=1, source_target_pairs={{0,16},{1,17},{2,18},{3,19},{4,20},{5,21},{6,22},{7,23},{8,24},{9,... | collective-permute-start | bytes 24584 | tf_op jit(solution)/shard_map/ppermute | solution.py:237
  33.7 1.2 collective-permute-done.1
  35.0 3.4 %collective-permute-start.2 = (f32[2,8,128]{2,1,0:T(8,128)S(1)}, f32[2,8,128]{2,1,0:T(8,128)S(1)}, u32[]{:S(2)}, u32[]{:S(2)}) collective-permute-start(f32[2,8,128]{2,1,0:T(8,128)S(1)} %broadcast_select_fusion.1), channel_id=1, source_target_pairs={{0,8},{1,9},{2,10},{3,11},{4,12},{5,13},{6,14},{7,15},{8,0},{9,1},... | collective-permute-start | bytes 24584 | tf_op jit(solution)/shard_map/ppermute | solution.py:237
  38.4 1.3 collective-permute-done.2
  39.7 4.8 %collective-permute-start.3 = (f32[4,4,128]{2,1,0:T(4,128)S(1)}, f32[4,4,128]{2,1,0:T(4,128)S(1)}, u32[]{:S(2)}, u32[]{:S(2)}) collective-permute-start(f32[4,4,128]{2,1,0:T(4,128)S(1)} %fusion.5), channel_id=1, source_target_pairs={{0,4},{1,5},{2,6},{3,7},{4,0},{5,1},{6,2},{7,3},{8,12},{9,13},{10,... | collective-permute-start | bytes 24584 | tf_op jit(solution)/shard_map/ppermute | solution.py:237
  44.6 1.1 collective-permute-done.3
  45.7 0.0 copy-start
  45.7 3.6 %collective-permute-start.4 = (f32[8,2,128]{2,0,1:T(8,128)S(1)}, f32[8,2,128]{2,0,1:T(8,128)S(1)}, u32[]{:S(2)}, u32[]{:S(2)}) collective-permute-start(f32[8,2,128]{2,0,1:T(8,128)S(1)} %fusion.4), channel_id=1, source_target_pairs={{0,2},{1,3},{2,0},{3,1},{4,6},{5,7},{6,4},{7,5},{8,10},{9,11},{10,... | collective-permute-start | bytes 24584 | tf_op jit(solution)/shard_map/ppermute | solution.py:237
  49.3 0.0 copy-start.1
  49.4 1.2 copy-done.1
  50.6 1.5 shard_map.66.prop_ref
  52.0 0.0 collective-permute-done.4
  52.1 3.0 %all-to-all-done.piece_ref = bf16[16,64,256]{2,1,0:T(8,128)(2,1)S(1)} async-done(((bf16[16,64,256]{2,1,0:T(8,128)(2,1)}), bf16[16,64,256]{2,1,0:T(8,128)(2,1)S(1)}, u32[]{:S(2)}, u32[]{:S(2)}) %all-to-all-start) | async-done | bytes 524320 | tf_op jit(solution)/shard_map/all_to_all | solution.py:281
  55.1 0.0 copy-done
  55.1 1.2 shard_map.65
  56.4 52.6 %all_to_all.20.piece_ref = bf16[512,2,256]{2,1,0:T(2,128)(2,1)S(1)} all-to-all(bf16[512,2,256]{2,1,0:T(2,128)(2,1)S(1)} %shard_map.65), channel_id=1, replica_groups=mesh['ra'=16,'rb'=32] {'ra','rb'}, dimensions={0} | all-to-all | bytes 1048576 | tf_op jit(solution)/shard_map/all_to_all | solution.py:288
  108.9 4.0 %shard_map.67 = bf16[512,2,256]{2,1,0:T(2,128)(2,1)S(1)} custom-call(bf16[512,2,256]{2,1,0:T(2,128)(2,1)S(1)} %all_to_all.20.piece_ref, bf16[2,512,512]{2,1,0:T(8,128)(2,1)S(1)} %shard_map.66.prop_ref, bf16[6,256,256]{2,1,0:T(8,128)(2,1)S(1)} %get-tuple-element.19.weights_ref, f32[32,128]{1,0:T(8,128)S(1)} %bitcast.86), custom_call_target="tpu_custom_call" | custom-call | tf_op jit(solution)/shard_map/pallas_call | solution.py:289
  113.0 44.1 %all_to_all.21.piece_ref = bf16[512,2,256]{2,1,0:T(2,128)(2,1)S(1)} all-to-all(bf16[512,2,256]{2,1,0:T(2,128)(2,1)S(1)} %shard_map.67), channel_id=1, replica_groups=mesh['ra'=16,'rb'=32] {'ra','rb'}, dimensions={0} | all-to-all | bytes 1048576 | tf_op jit(solution)/shard_map/all_to_all | solution.py:295
  157.1 1.5 shard_map.68
  158.6 29.9 %all_to_all.22.piece_ref = bf16[16,64,256]{2,1,0:T(8,128)(2,1)S(1)} all-to-all(bf16[16,64,256]{2,1,0:T(8,128)(2,1)S(1)} %shard_map.68), channel_id=1, replica_groups=mesh['ra'=16,'rb'=32] {'ra'}, dimensions={0} | all-to-all | bytes 1048576 | tf_op jit(solution)/shard_map/all_to_all | solution.py:301
  188.5 1.8 shard_map.69
  (19 shorter events, 0.1 us)
Async XLA Ops:
  0.9 16.4 %copy-start.4 = (f32[6,32,16]{1,2,0:T(8,128)S(1)}, f32[6,32,16]{1,2,0:T(8,128)}, u32[]{:S(2)}) copy-start(f32[6,32,16]{1,2,0:T(8,128)} %param.9) | copy-start | bytes 36868
  0.9 16.4 %copy-start.5 = (s32[6,4,4]{0,2,1:T(4,128)S(1)}, s32[6,4,4]{0,2,1:T(4,128)}, u32[]{:S(2)}) copy-start(s32[6,4,4]{0,2,1:T(4,128)} %param.8) | copy-start | bytes 1156
  0.9 28.1 %collective-permute-start = (f32[16,1,128]{2,0,1:T(8,128)S(1)}, f32[16,1,128]{2,0,1:T(8,128)S(1)}, u32[]{:S(2)}, u32[]{:S(2)}) collective-permute-start(f32[16,1,128]{2,0,1:T(8,128)S(1)} %broadcast_select_fusion), channel_id=1, source_target_pairs={{0,1},{1,0},{2,3},{3,2},{4,5},{5,4},{6,7},{7,6},{8,9},{9,8},{10,11... | collective-permute-start | bytes 24584 | tf_op jit(solution)/shard_map/ppermute | solution.py:237
  17.4 1.1 copy-start.2
  18.6 1.0 copy-start.3
  23.0 32.2 %all-to-all-start = ((bf16[16,64,256]{2,1,0:T(8,128)(2,1)}), bf16[16,64,256]{2,1,0:T(8,128)(2,1)S(1)}, u32[]{:S(2)}, u32[]{:S(2)}) async-start(bf16[16,64,256]{2,1,0:T(8,128)(2,1)} %get-tuple-element.13), calls=%async_computation | async-start | bytes 1048576 | tf_op jit(solution)/shard_map/all_to_all | solution.py:281
  29.0 5.9 %collective-permute-start.1 = (f32[1,16,128]{2,1,0:T(8,128)S(1)}, f32[1,16,128]{2,1,0:T(8,128)S(1)}, u32[]{:S(2)}, u32[]{:S(2)}) collective-permute-start(f32[1,16,128]{2,1,0:T(8,128)S(1)} %fusion.3), channel_id=1, source_target_pairs={{0,16},{1,17},{2,18},{3,19},{4,20},{5,21},{6,22},{7,23},{8,24},{9,... | collective-permute-start | bytes 24584 | tf_op jit(solution)/shard_map/ppermute | solution.py:237
  35.0 4.7 %collective-permute-start.2 = (f32[2,8,128]{2,1,0:T(8,128)S(1)}, f32[2,8,128]{2,1,0:T(8,128)S(1)}, u32[]{:S(2)}, u32[]{:S(2)}) collective-permute-start(f32[2,8,128]{2,1,0:T(8,128)S(1)} %broadcast_select_fusion.1), channel_id=1, source_target_pairs={{0,8},{1,9},{2,10},{3,11},{4,12},{5,13},{6,14},{7,15},{8,0},{9,1},... | collective-permute-start | bytes 24584 | tf_op jit(solution)/shard_map/ppermute | solution.py:237
  39.7 5.9 %collective-permute-start.3 = (f32[4,4,128]{2,1,0:T(4,128)S(1)}, f32[4,4,128]{2,1,0:T(4,128)S(1)}, u32[]{:S(2)}, u32[]{:S(2)}) collective-permute-start(f32[4,4,128]{2,1,0:T(4,128)S(1)} %fusion.5), channel_id=1, source_target_pairs={{0,4},{1,5},{2,6},{3,7},{4,0},{5,1},{6,2},{7,3},{8,12},{9,13},{10,... | collective-permute-start | bytes 24584 | tf_op jit(solution)/shard_map/ppermute | solution.py:237
  45.7 9.5 %copy-start = (bf16[2,512,512]{2,1,0:T(8,128)(2,1)S(1)}, bf16[2,512,512]{2,1,0:T(8,128)(2,1)}, u32[]{:S(2)}) copy-start(bf16[2,512,512]{2,1,0:T(8,128)(2,1)} %prop_ref.4) | copy-start | bytes 3145732
  45.7 6.3 %collective-permute-start.4 = (f32[8,2,128]{2,0,1:T(8,128)S(1)}, f32[8,2,128]{2,0,1:T(8,128)S(1)}, u32[]{:S(2)}, u32[]{:S(2)}) collective-permute-start(f32[8,2,128]{2,0,1:T(8,128)S(1)} %fusion.4), channel_id=1, source_target_pairs={{0,2},{1,3},{2,0},{3,1},{4,6},{5,7},{6,4},{7,5},{8,10},{9,11},{10,... | collective-permute-start | bytes 24584 | tf_op jit(solution)/shard_map/ppermute | solution.py:237
  49.3 1.2 copy-start.1
